TPU v7x, 512 devices: a whole 4x4x16 slice. The times are simulated.
512 devices in a mesh: seq: 128 (over z, y, core), head: 4 (over x).
Axes of the slice: x: 4, y: 4, z: 16, core: 2. Of those that a mesh axis runs over, the one named last changes fastest.
Arguments:
- queries: bfloat16 [65536, 2048], P('seq', 'head'), may hold values from -6 to 6
- keys: bfloat16 [65536, 2048], P('seq', 'head'), may hold values from -6 to 6
- values: bfloat16 [65536, 2048], P('seq', 'head'), may hold values from -6 to 6
- out_grad: bfloat16 [65536, 2048], P('seq', 'head'), may hold values from -6 to 6
- labels: int32 [8, 65536, 1], P('head', 'seq'), may hold values from 0 to 511; in each aligned block of 512 rows (0 to 511, 512 to 1023, ..., all dimensions but the last counted through in order) at most 4 rows name the same one
Outputs:
- attended: bfloat16 [65536, 2048], P('seq', 'head')
- grad_queries: bfloat16 [65536, 2048], P('seq', 'head')
- grad_keys: bfloat16 [65536, 2048], P('seq', 'head')
- grad_values: bfloat16 [65536, 2048], P('seq', 'head')
Inputs may be any that keep to these rules, and one draw needn't show every extreme that they name: `labels`: in each routed head the 512 tokens of one device name no cluster more than 4 times, and in some device some cluster is named exactly 4 times.
All inputs are finite; a program needn't handle non-finite values.
Results may differ from a plain program's by a relative error of at most 0.039.
Values may be sent and summed in bfloat16 or wider, within the bound.
No kernel may reach another device: no remote copies, remote signals or barrier semaphores. Data moves between devices by JAX's collectives and lax.ppermute only.
A program may use at most 128 MiB of HBM per device.

v0:
```python
import math

import jax
import jax.numpy as jnp
from jax import lax
from jax.sharding import PartitionSpec as P

HD = 128
CLUSTERS = 512
WINDOW = 256
SLOTS = 4


MASKED = -1e30


def passed_along(value, axis, steps):
    count = lax.axis_size(axis)
    leading, last = (max(0, -steps), min(count, count - steps))
    return lax.ppermute(value, axis, [(source, source + steps) for source in range(leading, last)])


def forward_pass(queries_in, key_rows, value_rows, keep_mask):
    factor = 1.0 / math.sqrt(queries_in.shape[-1])
    scores = (
        jnp.einsum("...rd,...cd->...rc", queries_in, key_rows, preferred_element_type=jnp.float32)
        * factor
    )
    scores = jnp.where(keep_mask, scores, MASKED)
    row_max = jnp.max(scores, axis=-1, keepdims=True)
    raised = jnp.exp(scores - row_max)
    weights = raised / jnp.sum(raised, axis=-1, keepdims=True)
    rounded = weights.astype(jnp.bfloat16)
    output = jnp.einsum(
        "...rc,...cd->...rd", rounded, value_rows, preferred_element_type=jnp.float32
    ).astype(jnp.bfloat16)
    return (weights, rounded, output)


def backward_pass(queries_in, key_rows, value_rows, grad_rows, weights, rounded, output):
    factor = 1.0 / math.sqrt(queries_in.shape[-1])
    row_dot = jnp.sum(
        grad_rows.astype(jnp.float32) * output.astype(jnp.float32), axis=-1, keepdims=True
    )
    grad_weight = jnp.einsum(
        "...rd,...cd->...rc", grad_rows, value_rows, preferred_element_type=jnp.float32
    )
    grad_score = (weights * (grad_weight - row_dot) * factor).astype(jnp.bfloat16)
    grad_query = jnp.einsum(
        "...rc,...cd->...rd", grad_score, key_rows, preferred_element_type=jnp.float32
    )
    grad_key = jnp.einsum(
        "...rc,...rd->...cd", grad_score, queries_in, preferred_element_type=jnp.float32
    )
    grad_value = jnp.einsum(
        "...rc,...rd->...cd", rounded, grad_rows, preferred_element_type=jnp.float32
    )
    return (grad_query, grad_key, grad_value)


def window_mask(query_pos, key_pos):
    later = key_pos[None, :] <= query_pos[:, None]
    inside = key_pos[None, :] >= query_pos[:, None] - WINDOW
    return later & inside & (key_pos[None, :] >= 0)


def heads_first(rows):
    return jnp.transpose(rows, (1, 0, 2))


def cluster_mask(token_pos):
    block_rows = token_pos.shape[-1]
    later = (token_pos[..., None, :] >= 0) & (token_pos[..., None, :] <= token_pos[..., :, None])
    return later | jnp.eye(block_rows, dtype=bool)


def merge_slots(blocks):
    lead = blocks.shape
    return blocks.reshape((lead[0], lead[1] * lead[2]) + lead[3:])


def forward_head(packed):
    rows, token_pos = packed
    flat = merge_slots(rows)
    keep_mask = cluster_mask(merge_slots(token_pos))
    weights, rounded, output = forward_pass(
        flat[..., :HD], flat[..., HD : 2 * HD], flat[..., 2 * HD :], keep_mask
    )
    return output


def backward_head(packed):
    rows, token_pos, grad_rows, out_rows = packed
    flat = merge_slots(rows)
    keep_mask = cluster_mask(merge_slots(token_pos))
    query_blk = flat[..., :HD]
    key_blk = flat[..., HD : 2 * HD]
    value_blk = flat[..., 2 * HD :]
    weights, rounded, again = forward_pass(query_blk, key_blk, value_blk, keep_mask)
    grad_query, grad_key, grad_value = backward_pass(
        query_blk, key_blk, value_blk, merge_slots(grad_rows), weights, rounded, out_rows
    )
    return jnp.concatenate(
        [
            grad_query.astype(jnp.bfloat16),
            grad_key.astype(jnp.bfloat16),
            grad_value.astype(jnp.bfloat16),
        ],
        axis=-1,
    )


def local(queries, keys, values, out_grad, labels):
    tok_rows = queries.shape[0]
    half_cols = queries.shape[1] // 2
    seq_count = lax.axis_size("seq")
    cluster_dev = CLUSTERS // seq_count
    first_pos = lax.axis_index("seq") * tok_rows
    row_rank = jnp.arange(tok_rows, dtype=jnp.int32)
    query_pos = first_pos + row_rank
    local_q, local_k, local_v, local_g = [
        source[:, :half_cols].reshape(tok_rows, 2, HD)
        for source in (queries, keys, values, out_grad)
    ]
    routed_q, routed_k, routed_v, routed_g = [
        source[:, half_cols:].reshape(tok_rows, 2, HD)
        for source in (queries, keys, values, out_grad)
    ]
    clusters = labels[:, :, 0]
    same = clusters[:, :, None] == clusters[:, None, :]
    earlier = row_rank[None, :] < row_rank[:, None]
    slot_rank = jnp.sum(same & earlier[None], axis=-1)
    owners = clusters // cluster_dev
    within = clusters % cluster_dev
    head_rank = jnp.arange(2, dtype=jnp.int32)[:, None]

    def place(rows):
        empty = jnp.zeros((2, cluster_dev, seq_count, SLOTS, rows.shape[-1]), rows.dtype)
        return empty.at[head_rank, within, owners, slot_rank].set(jnp.transpose(rows, (1, 0, 2)))

    pos_buf = jnp.full((2, cluster_dev, seq_count, SLOTS), -1, jnp.int32)
    pos_buf = pos_buf.at[head_rank, within, owners, slot_rank].set(
        jnp.broadcast_to(query_pos[None], (2, tok_rows))
    )
    sent = place(jnp.concatenate([routed_q, routed_k, routed_v], axis=-1))
    got_rows, got_pos = (
        lax.all_to_all(sent, "seq", split_axis=2, concat_axis=2, tiled=True),
        lax.all_to_all(pos_buf, "seq", split_axis=2, concat_axis=2, tiled=True),
    )
    lead = got_rows.shape
    output = lax.map(forward_head, (got_rows, got_pos))
    out_back = lax.all_to_all(
        output.reshape(lead[:4] + (HD,)), "seq", split_axis=2, concat_axis=2, tiled=True
    )
    got_grad = lax.all_to_all(place(routed_g), "seq", split_axis=2, concat_axis=2, tiled=True)
    grads_now = lax.map(backward_head, (got_rows, got_pos, got_grad, output)).reshape(
        lead[:4] + (3 * HD,)
    )
    grads_home = lax.all_to_all(grads_now, "seq", split_axis=2, concat_axis=2, tiled=True)
    results = jnp.concatenate([out_back, grads_home], axis=-1)
    tail_rows = jnp.concatenate(
        [local_k[tok_rows - WINDOW :], local_v[tok_rows - WINDOW :]], axis=1
    )
    before = passed_along(tail_rows, "seq", 1)
    key_all = jnp.concatenate([before[:, :2], local_k], axis=0)
    value_all = jnp.concatenate([before[:, 2:], local_v], axis=0)
    key_pos = first_pos - WINDOW + jnp.arange(WINDOW + tok_rows, dtype=jnp.int32)
    keep_local = window_mask(query_pos, key_pos)[None]
    head_q = heads_first(local_q)
    head_k = heads_first(key_all)
    head_v = heads_first(value_all)
    head_g = heads_first(local_g)
    weights_l, rounded_l, local_out = forward_pass(head_q, head_k, head_v, keep_local)
    local_gq, grad_key_all, grad_value_all = backward_pass(
        head_q, head_k, head_v, head_g, weights_l, rounded_l, local_out
    )
    own_key = grad_key_all[:, WINDOW:]
    own_value = grad_value_all[:, WINDOW:]
    edge_rows = jnp.concatenate([grad_key_all[:, :WINDOW], grad_value_all[:, :WINDOW]], axis=0)
    after = passed_along(edge_rows.astype(jnp.bfloat16), "seq", -1).astype(edge_rows.dtype)
    extra_key = after[:2]
    extra_value = after[2:]
    own_key = own_key.at[:, tok_rows - WINDOW :].add(extra_key)
    own_value = own_value.at[:, tok_rows - WINDOW :].add(extra_value)
    picked = jnp.transpose(results[head_rank, within, owners, slot_rank], (1, 0, 2))

    def combine(local_heads, column_block):
        routed_heads = picked[:, :, column_block * HD : (column_block + 1) * HD]
        return jnp.concatenate([heads_first(local_heads), routed_heads], axis=1).reshape(
            tok_rows, 2 * half_cols
        )

    return (
        combine(local_out, 0),
        combine(local_gq.astype(jnp.bfloat16), 1),
        combine(own_key.astype(jnp.bfloat16), 2),
        combine(own_value.astype(jnp.bfloat16), 3),
    )


def solution(mesh):
    in_specs = (
        P("seq", "head"),
        P("seq", "head"),
        P("seq", "head"),
        P("seq", "head"),
        P("head", "seq", None),
    )
    out_specs = (P("seq", "head"), P("seq", "head"), P("seq", "head"), P("seq", "head"))
    return jax.shard_map(local, mesh=mesh, in_specs=in_specs, out_specs=out_specs, check_vma=False)
```

profile of v0, /device:TPU:127, one launch (start us, length us, event | category | flops | bytes accessed | tf_op | source)
XLA Modules:
  0.0 550.2 jit_solution(7999870944044200082)
XLA Ops:
  5.7 4.3 scatter_custom_fusion
  11.0 18.8 %all-to-all-start = ((s32[2,4,128,4]{3,1,0,2:T(4,128)}), s32[2,4,128,4]{3,1,0,2:T(4,128)}, u32[]{:S(2)}, u32[]{:S(2)}) async-start(s32[2,4,128,4]{3,1,0,2:T(4,128)} %copy.231), calls=%async_computation | async-start | bytes 1048576 | tf_op jit(solution)/shard_map/all_to_all | solution.py:148
  29.8 1.8 fusion.116
  34.8 6.6 %scatter_custom_fusion.1 = bf16[4096,384]{1,0:T(8,128)(2,1)S(1)} fusion(s32[1024]{0:T(1024)S(1)} %bitcast.181, bf16[1024,384]{1,0:T(8,128)(2,1)} %bitcast.172, bf16[]{:T(256)} %constant.146.clone.1), kind=kCustom, calls=%fused_computation.82 | custom fusion | bytes 3146240
  41.4 2.5 reshape.330
  43.8 4.6 copy.236
  48.5 10.8 %all-to-all-done = s32[2,4,128,4]{3,1,0,2:T(4,128)} async-done(((s32[2,4,128,4]{3,1,0,2:T(4,128)}), s32[2,4,128,4]{3,1,0,2:T(4,128)}, u32[]{:S(2)}, u32[]{:S(2)}) %all-to-all-start) | async-done | bytes 16416 | tf_op jit(solution)/shard_map/all_to_all | solution.py:148
  59.3 10.1 %all-to-all-start.1 = ((bf16[2,4,128,4,384]{4,3,1,0,2:T(4,128)(2,1)}), bf16[2,4,128,4,384]{4,3,1,0,2:T(4,128)(2,1)S(1)}, u32[]{:S(2)}, u32[]{:S(2)}) async-start(bf16[2,4,128,4,384]{4,3,1,0,2:T(4,128)(2,1)} %copy.236), calls=%async_computation.1 | async-start | bytes 6291456 | tf_op jit(solution)/shard_map/all_to_all | solution.py:147
  69.4 1.9 fusion.115
  73.2 4.6 scatter_custom_fusion.2
  77.8 2.6 copy.242
  80.4 130.0 %all-to-all-done.1 = bf16[2,4,128,4,384]{4,3,1,0,2:T(4,128)(2,1)S(1)} async-done(((bf16[2,4,128,4,384]{4,3,1,0,2:T(4,128)(2,1)}), bf16[2,4,128,4,384]{4,3,1,0,2:T(4,128)(2,1)S(1)}, u32[]{:S(2)}, u32[]{:S(2)}) %all-to-all-start.1) | async-done | bytes 3145760 | tf_op jit(solution)/shard_map/all_to_all | solution.py:147
  210.3 11.5 %all-to-all-start.3 = ((bf16[2,4,128,4,128]{4,3,1,0,2:T(4,128)(2,1)}), bf16[2,4,128,4,128]{4,3,1,0,2:T(4,128)(2,1)}, u32[]{:S(2)}, u32[]{:S(2)}) async-start(bf16[2,4,128,4,128]{4,3,1,0,2:T(4,128)(2,1)} %copy.242), calls=%async_computation.3 | async-start | bytes 2097152 | tf_op jit(solution)/shard_map/all_to_all | solution.py:155
  221.9 1.9 copy.237
  223.9 2.9 copy.238
  226.8 20.8 %while.22 = (s32[]{:T(128)}, bf16[2,4,512,128]{3,2,1,0:T(8,128)(2,1)}, s32[2,4,128,4]{3,2,1,0:T(8,128)}, bf16[2,4,128,4,384]{4,3,2,1,0:T(4,128)(2,1)}, s32[]{:T(128)}) while((s32[]{:T(128)}, bf16[2,4,512,128]{3,2,1,0:T(8,128)(2,1)}, s32[2,4,128,4]{3,2,1,0:T(8,128)}, bf16[2,4,128,4,384]{4,3,2,1,0:T(4,128)(2,1)}, s32[]{:T(128)}) %tuple.80), condition=%wide.region_8.9_spmd, body=%wide.region_5.8_spmd.sunk | while | flops 821564416 | bytes 18708616 | solution.py:151
  228.0 2.0 constant_dynamic-slice_fusion.15
  230.4 2.5 fusion.163
  232.9 3.3 fusion.164
  238.4 2.0 constant_dynamic-slice_fusion.15
  240.8 2.5 fusion.163
  243.3 3.3 fusion.164
  247.5 2.6 copy.239
  250.2 23.2 %all-to-all-done.3 = bf16[2,4,128,4,128]{4,3,1,0,2:T(4,128)(2,1)} async-done(((bf16[2,4,128,4,128]{4,3,1,0,2:T(4,128)(2,1)}), bf16[2,4,128,4,128]{4,3,1,0,2:T(4,128)(2,1)}, u32[]{:S(2)}, u32[]{:S(2)}) %all-to-all-start.3) | async-done | bytes 1048608 | tf_op jit(solution)/shard_map/all_to_all | solution.py:155
  273.4 10.7 %all-to-all-start.2 = ((bf16[2,4,128,4,128]{4,3,1,0,2:T(4,128)(2,1)}), bf16[2,4,128,4,128]{4,3,1,0,2:T(4,128)(2,1)}, u32[]{:S(2)}, u32[]{:S(2)}) async-start(bf16[2,4,128,4,128]{4,3,1,0,2:T(4,128)(2,1)} %copy.239), calls=%async_computation.2 | async-start | bytes 2097152 | tf_op jit(solution)/shard_map/all_to_all | solution.py:152
  284.1 44.7 %while.23 = (s32[]{:T(128)}, bf16[2,4,512,384]{3,1,2,0:T(4,128)(2,1)}, s32[2,4,128,4]{3,2,1,0:T(8,128)}, bf16[2,4,128,4,384]{4,3,2,1,0:T(4,128)(2,1)}, bf16[2,4,...) while((s32[]{:T(128)}, bf16[2,4,512,384]{3,1,2,0:T(4,128)(2,1)}, ...), condition=%wide.region_14.15_spmd, body=%wide.region_10.14_spmd.sunk | while | flops 1363673600 | bytes 50974884 | solution.py:156
  287.5 2.0 constant_dynamic-slice_fusion.19
  289.9 3.8 fusion.175
  293.7 3.1 fusion.176
  296.9 1.7 fusion.177
  298.8 3.0 multiply_convert_fusion.2
  303.2 1.4 copy.314
  304.7 1.8 constant_dynamic-update-slice_fusion.2
  309.9 2.0 constant_dynamic-slice_fusion.19
  312.3 3.8 fusion.175
  316.1 3.1 fusion.176
  319.3 1.7 fusion.177
  321.2 3.0 multiply_convert_fusion.2
  325.6 1.4 copy.314
  327.1 1.7 constant_dynamic-update-slice_fusion.2
  328.8 5.2 copy.247
  334.0 1.6 all-to-all-done.2
  335.6 14.7 %all-to-all-start.4 = ((bf16[2,4,128,4,384]{4,3,1,0,2:T(4,128)(2,1)}), bf16[2,4,128,4,384]{4,3,1,0,2:T(4,128)(2,1)S(1)}, u32[]{:S(2)}, u32[]{:S(2)}) async-start(bf16[2,4,128,4,384]{4,3,1,0,2:T(4,128)(2,1)} %copy.247), calls=%async_computation.4 | async-start | bytes 6291456 | tf_op jit(solution)/shard_map/all_to_all | solution.py:159
  350.2 1.6 slice.146
  352.7 1.7 copy.288
  354.4 1.7 copy.219
  357.9 1.6 pad_maximum_fusion.5
  359.5 4.8 collective-permute-start
  367.2 1.8 copy.289
  368.9 1.8 copy.221
  370.7 1.8 copy.224
  373.7 114.2 %collective-permute-done = bf16[256,4,128]{2,0,1:T(8,128)(2,1)} collective-permute-done((bf16[256,4,128]{2,0,1:T(8,128)(2,1)}, bf16[256,4,128]{2,0,1:T(8,128)(2,1)}, u32[]{:S(2)}, u32[]{:S(2)}) %collective-permute-start) | collective-permute-done | bytes 262176 | tf_op jit(solution)/shard_map/ppermute | solution.py:20
  487.9 1.6 fusion.119
  489.5 4.2 fusion.120
  493.7 2.4 fusion.78
  499.0 1.7 copy.225
  500.6 2.7 multiply_reduce_fusion
  503.3 2.8 fusion.71
  506.9 1.9 collective-permute-start.1
  509.9 9.0 %collective-permute-done.1 = bf16[4,256,128]{1,2,0:T(8,128)(2,1)S(1)} collective-permute-done((bf16[4,256,128]{1,2,0:T(8,128)(2,1)S(1)}, bf16[4,256,128]{1,2,0:T(8,128)(2,1)S(1)}, u32[]{:S(2)}, u32[]{:S(2)}) %collective-permute-start.1) | collective-permute-done | bytes 262176 | tf_op jit(solution)/shard_map/ppermute | solution.py:20
  518.9 1.7 fusion.84
  520.6 3.8 pad_maximum_fusion
  524.4 3.6 copy.279
  528.0 15.7 %gather_fusion = bf16[1024,512]{1,0:T(8,128)(2,1)S(1)} fusion(bf16[2,4,128,4,512]{4,3,2,1,0:T(4,128)(2,1)} %copy.279, s32[1024]{0:T(1024)S(1)} %bitcast.149), kind=kCustom, calls=%fused_computation | custom fusion | bytes 2113536 | tf_op jit(solution)/shard_map/gather | solution.py:185
  (135 shorter events, 44.8 us)
Async XLA Ops:
  0.6 31.1 %copy-start.8 = (bf16[512,512]{1,0:T(8,128)(2,1)S(1)}, bf16[512,512]{1,0:T(8,128)(2,1)}, u32[]{:S(2)}) copy-start(bf16[512,512]{1,0:T(8,128)(2,1)} %param.14) | copy-start | bytes 1572868
  0.6 32.0 %copy-start.9 = (bf16[512,512]{1,0:T(8,128)(2,1)S(1)}, bf16[512,512]{1,0:T(8,128)(2,1)}, u32[]{:S(2)}) copy-start(bf16[512,512]{1,0:T(8,128)(2,1)} %param.13) | copy-start | bytes 1572868
  5.7 25.9 %copy-start.15 = (s32[512]{0:T(512)}, s32[512]{0:T(512)S(1)}, u32[]{:S(2)}) copy-start(s32[512]{0:T(512)S(1)} %get-tuple-element.209) | copy-start | bytes 6148
  11.0 48.3 %all-to-all-start = ((s32[2,4,128,4]{3,1,0,2:T(4,128)}), s32[2,4,128,4]{3,1,0,2:T(4,128)}, u32[]{:S(2)}, u32[]{:S(2)}) async-start(s32[2,4,128,4]{3,1,0,2:T(4,128)} %copy.231), calls=%async_computation | async-start | bytes 1048576 | tf_op jit(solution)/shard_map/all_to_all | solution.py:148
  59.3 151.1 %all-to-all-start.1 = ((bf16[2,4,128,4,384]{4,3,1,0,2:T(4,128)(2,1)}), bf16[2,4,128,4,384]{4,3,1,0,2:T(4,128)(2,1)S(1)}, u32[]{:S(2)}, u32[]{:S(2)}) async-start(bf16[2,4,128,4,384]{4,3,1,0,2:T(4,128)(2,1)} %copy.236), calls=%async_computation.1 | async-start | bytes 6291456 | tf_op jit(solution)/shard_map/all_to_all | solution.py:147
  210.3 63.0 %all-to-all-start.3 = ((bf16[2,4,128,4,128]{4,3,1,0,2:T(4,128)(2,1)}), bf16[2,4,128,4,128]{4,3,1,0,2:T(4,128)(2,1)}, u32[]{:S(2)}, u32[]{:S(2)}) async-start(bf16[2,4,128,4,128]{4,3,1,0,2:T(4,128)(2,1)} %copy.242), calls=%async_computation.3 | async-start | bytes 2097152 | tf_op jit(solution)/shard_map/all_to_all | solution.py:155
  230.4 2.5 copy-start.1
  236.2 1.0 copy-start.2
  240.7 2.5 copy-start.1
  246.6 1.0 copy-start.2
  273.4 62.2 %all-to-all-start.2 = ((bf16[2,4,128,4,128]{4,3,1,0,2:T(4,128)(2,1)}), bf16[2,4,128,4,128]{4,3,1,0,2:T(4,128)(2,1)}, u32[]{:S(2)}, u32[]{:S(2)}) async-start(bf16[2,4,128,4,128]{4,3,1,0,2:T(4,128)(2,1)} %copy.239), calls=%async_computation.2 | async-start | bytes 2097152 | tf_op jit(solution)/shard_map/all_to_all | solution.py:152
  289.9 3.8 copy-start
  293.7 3.1 copy-start.3
  312.3 3.8 copy-start
  316.1 3.1 copy-start.3
  334.0 30.4 %copy-start.17 = (s32[1,4,2,128]{3,2,1,0:T(2,128)S(1)}, s32[1,4,2,128]{3,2,1,0:T(2,128)}, u32[]{:S(2)}) copy-start(s32[1,4,2,128]{3,2,1,0:T(2,128)} %get-tuple-element.180) | copy-start | bytes 12292
  334.0 30.4 %copy-start.7 = (bf16[512,256]{1,0:T(8,128)(2,1)S(1)}, bf16[512,256]{1,0:T(8,128)(2,1)}, u32[]{:S(2)}) copy-start(bf16[512,256]{1,0:T(8,128)(2,1)} %get-tuple-element.192) | copy-start | bytes 786436
  335.6 185.1 %all-to-all-start.4 = ((bf16[2,4,128,4,384]{4,3,1,0,2:T(4,128)(2,1)}), bf16[2,4,128,4,384]{4,3,1,0,2:T(4,128)(2,1)S(1)}, u32[]{:S(2)}, u32[]{:S(2)}) async-start(bf16[2,4,128,4,384]{4,3,1,0,2:T(4,128)(2,1)} %copy.247), calls=%async_computation.4 | async-start | bytes 6291456 | tf_op jit(solution)/shard_map/all_to_all | solution.py:159
  350.2 22.3 %copy-start.16 = (s32[512]{0:T(512)S(1)}, s32[512]{0:T(512)}, u32[]{:S(2)}) copy-start(s32[512]{0:T(512)} %copy-done.15) | copy-start | bytes 6148
  350.2 22.3 %copy-start.18 = (s32[512]{0:T(512)S(1)}, s32[512]{0:T(512)}, u32[]{:S(2)}) copy-start(s32[512]{0:T(512)} %get-tuple-element.210) | copy-start | bytes 6148
  359.5 128.4 %collective-permute-start = (bf16[256,4,128]{2,0,1:T(8,128)(2,1)}, bf16[256,4,128]{2,0,1:T(8,128)(2,1)}, u32[]{:S(2)}, u32[]{:S(2)}) collective-permute-start(bf16[256,4,128]{2,0,1:T(8,128)(2,1)} %pad_maximum_fusion.5), channel_id=1, source_target_pairs={{0,4},{4,8},{8,12},{12,16},{16,20},{20,24},{24,28},{28,32},{32,36}... | collective-permute-start | bytes 786440 | tf_op jit(solution)/shard_map/ppermute | solution.py:20
  489.5 4.2 copy-start.13
  493.7 3.5 copy-start.6
  496.1 1.1 copy-start.4
  497.9 1.0 copy-start.5
  506.1 2.7 copy-start.10
  506.1 2.7 copy-start.14
  506.9 12.0 %collective-permute-start.1 = (bf16[4,256,128]{1,2,0:T(8,128)(2,1)S(1)}, bf16[4,256,128]{1,2,0:T(8,128)(2,1)S(1)}, u32[]{:S(2)}, u32[]{:S(2)}) collective-permute-start(bf16[4,256,128]{1,2,0:T(8,128)(2,1)S(1)} %pad_maximum_fusion.6), channel_id=1, source_target_pairs={{4,0},{8,4},{12,8},{16,12},{20,16},{24,20},{28,24},{32,28},{36,32}... | collective-permute-start | bytes 786440 | tf_op jit(solution)/shard_map/ppermute | solution.py:20
  543.6 1.0 copy-start.11
  543.7 2.0 copy-start.12
where the time goes:
time: 561 us; the launch traced here: 550 us
  waiting for transfers between devices  289 us (52%)
  local copies, waits for them, and re-layouts  121 us (22%)
  starting transfers between devices  72.5 us (13%)
  matrix products  46.2 us (8%)
  other arithmetic  20.1 us (4%)
    all_to_all x1, waiting for transfers between devices, local(): lax.all_to_all(sent, 'seq', split_axis=2, concat_axis=2, tiled=True)  130 us
    ppermute x2, waiting for transfers between devices, passed_along(): lax.ppermute(value, axis, [(source, source + steps) for source in range(l...  123 us
    unnamed x51, local copies, waits for them, and re-layouts  28.9 us
    all_to_all x1, waiting for transfers between devices, local(): lax.all_to_all(place(routed_g), 'seq', split_axis=2, concat_axis=2, tiled...  23.2 us
    all_to_all x1, starting transfers between devices, local(): lax.all_to_all(pos_buf, 'seq', split_axis=2, concat_axis=2, tiled=True)  18.8 us
    sub x5, matrix products, forward_pass(): raised = jnp.exp(scores - row_max)  16.9 us
    gather x2, local copies, waits for them, and re-layouts, local(): results[head_rank, within, owners, slot_rank]  16.2 us
    all_to_all x1, starting transfers between devices, local(): lax.all_to_all(grads_now, 'seq', split_axis=2, concat_axis=2, tiled=True)  14.7 us
  transfers between devices with their start and end apart: 7, of which 6 were waited for; matrix products, arithmetic and copies ran while one was open for 26% of the time, Pallas kernels for 0%

commit v1 on v0

v1 whole, which is shorter than its diff:
```python
import math

import jax
import jax.numpy as jnp
from jax import lax
from jax.experimental import pallas as pl
from jax.experimental.pallas import tpu as pltpu
from jax.sharding import PartitionSpec as P

HD = 128
CLUSTERS = 512
WINDOW = 256
TOK = 512
DEVS = 128
CAP = 12
NEAR = 8 * DEVS
WIDE = 6 * HD
GROUP = 384
GROUPS = 4
ROWS = GROUP * GROUPS
PARTS = 10
TRIES = 64
TURNS = ((37, 11), (59, 77), (83, 40), (101, 95), (29, 23), (71, 118))
BLOCK = 256
MASKED = -1e30
FACTOR = 1.0 / math.sqrt(HD)
BF = jnp.bfloat16
F32 = jnp.float32

NN = (((1,), (0,)), ((), ()))
NT = (((1,), (1,)), ((), ()))
TN = (((0,), (0,)), ((), ()))


def dot(a, b, dims=NN):
    return lax.dot_general(a, b, dims, preferred_element_type=F32)


def iota(shape, dim):
    return lax.broadcasted_iota(jnp.int32, shape, dim)


def ones_where(condition):
    return jnp.where(condition, 1.0, 0.0)


def shape(dims, kind=BF):
    return jax.ShapeDtypeStruct(dims, kind)


VMEM = pl.BlockSpec(memory_space=pltpu.VMEM)
SMEM = pl.BlockSpec(memory_space=pltpu.SMEM)
ANY = pl.BlockSpec(memory_space=pl.ANY)


def call(
    kernel, out_shape, in_specs, out_specs, scratch=(), flops=0, moved=0, aliases=None, grid=()
):
    return pl.pallas_call(
        kernel,
        grid=grid,
        out_shape=out_shape,
        in_specs=in_specs,
        out_specs=out_specs,
        scratch_shapes=list(scratch),
        input_output_aliases=aliases or {},
        compiler_params=pltpu.CompilerParams(vmem_limit_bytes=48 * 2**20),
        cost_estimate=pl.CostEstimate(flops=flops, bytes_accessed=moved, transcendentals=0),
    )


def low_half():
    return (iota((128, 2 * HD), 0) & 7) < 4


def fold(rows):
    first, second = rows[:, : 2 * HD], rows[:, 2 * HD :]
    low = low_half()
    even = jnp.where(low, first, pltpu.roll(second, 4, 0))
    odd = jnp.where(low, pltpu.roll(first, 124, 0), second)
    both = [part.reshape(16, 8, 2 * HD) for part in (even, odd)]
    return jnp.stack(both, axis=1).reshape(2 * 128, 2 * HD).astype(BF)


def unfold(rows):
    both = rows.astype(F32).reshape(16, 2, 8, 2 * HD)
    even = both[:, 0].reshape(128, 2 * HD)
    odd = both[:, 1].reshape(128, 2 * HD)
    low = low_half()
    first = jnp.where(low, even, pltpu.roll(odd, 4, 0))
    second = jnp.where(low, pltpu.roll(even, 124, 0), odd)
    return jnp.concatenate([first, second], axis=1).astype(BF)


def spread_out(buffer_ref, rows_ref):
    for i in range(GROUPS):
        near = slice(i * BLOCK, (i + 1) * BLOCK)
        rows_ref[i * GROUP : i * GROUP + BLOCK, :] = buffer_ref[near, : 4 * HD]
        rows_ref[i * GROUP + BLOCK : (i + 1) * GROUP, :] = unfold(buffer_ref[near, 4 * HD :])


def tail_kernel(k_ref, v_ref, tail_ref):
    half = 2 * HD
    tail_ref[:, :half] = k_ref[:, :half]
    tail_ref[:, half:] = v_ref[:, :half]


def count_kernel(labels_ref, counts_ref, within_ref):
    later = ones_where(iota((TOK, TOK), 0) < iota((TOK, TOK), 1)).astype(BF)
    rows = []
    within_ref[...] = jnp.zeros_like(within_ref)
    for h in range(2):
        hit = ones_where(labels_ref[h] == iota((CLUSTERS, TOK), 0))
        total = dot(jnp.ones((8, TOK), BF), hit.astype(BF), NT)
        rows += [total[0:1, k * 128 : (k + 1) * 128] for k in range(4)]
        before = dot(hit.astype(BF), later)
        within_ref[h : h + 1, :] = jnp.sum(hit * before, axis=0, keepdims=True)
    table = jnp.concatenate(rows, axis=0)
    counts_ref[...] = jnp.broadcast_to(table[None], (DEVS, 8, 128)).astype(BF)


def shifts_of(attempt):
    return [(attempt * a + b) & 127 for a, b in TURNS]


def dealt(ranked, attempt):
    shifts = shifts_of(attempt)
    lane = iota((DEVS, 128), 1)
    wide = jnp.where((attempt & 1) == 0, 24, 0)
    lists = []
    for h in range(2):
        lists.append(pltpu.roll(ranked[4 * h], 64, 1) if h else ranked[4 * h])
        lists += [pltpu.roll(ranked[4 * h + k], shifts[3 * h + k - 1], 1) for k in (1, 2)]
        final = pltpu.roll(ranked[4 * h + 3], shifts[3 * h + 2], 1)
        passed = (lane >= 64 * h) & (lane < 64 * h + wide)
        lists.append(jnp.where(passed, 0.0, final))
        lists.append(pltpu.roll(jnp.where(passed, final, 0.0), 32, 1))
    return lists


def place_kernel(
    where_ref, counts_ref, labels_ref, within_ref, q_ref, k_ref, v_ref, g_ref,
    send_ref, slot_ref, name_ref, over_ref, table, ranked, stage, sems,
):
    me = where_ref[0]
    mode = where_ref[1]
    table[...] = counts_ref[...].astype(F32).reshape(DEVS * 8, 128)
    per = [table[pl.ds(r, DEVS, stride=8), :] for r in range(8)]
    orders = []
    for h in range(2):
        key_row, key_col = [], []
        for k in range(4):
            block = per[4 * h + k]
            down = jnp.sum(block, axis=0, keepdims=True)
            across = jnp.sum(block.T, axis=1, keepdims=True)
            tie_row = (CLUSTERS - 1 - k * 128) - iota((1, 128), 1)
            tie_col = (CLUSTERS - 1 - k * 128) - iota((128, 1), 0)
            key_row.append(down * CLUSTERS + tie_row.astype(F32))
            key_col.append(across * CLUSTERS + tie_col.astype(F32))
        order = []
        for k in range(4):
            larger = jnp.zeros((128, 128), F32)
            for other in range(4):
                larger = larger + ones_where(key_col[other] > key_row[k])
            rank = jnp.sum(larger, axis=0, keepdims=True).astype(jnp.int32)
            order.append(ones_where(iota((CLUSTERS, 128), 0) == rank).astype(BF))
        amount = sum(dot(per[4 * h + k].astype(BF), order[k], NT) for k in range(4))
        for k in range(4):
            ranked[4 * h + k] = amount[:, k * 128 : (k + 1) * 128]
        orders.append(jnp.concatenate(order, axis=1))

    def unfit(state):
        attempt, most = state
        return jnp.logical_and(most > CAP, attempt < TRIES)

    def attempt_next(state):
        attempt, _ = state
        return attempt + 1, jnp.max(sum(dealt(ranked, attempt)))

    attempt, most = lax.while_loop(unfit, attempt_next, (jnp.int32(0), jnp.float32(CAP + 1)))
    attempt = attempt - 1
    over = most > CAP
    over_ref[...] = jnp.full((8, 128), jnp.where(over, 1.0, 0.0), F32)

    amounts = dealt(ranked, attempt)
    offsets = [jnp.zeros((DEVS, 128), F32)]
    for j in range(PARTS):
        offsets.append(offsets[-1] + amounts[j])
    begin = 3 * mode
    end = jnp.where(over, jnp.minimum(begin + 3, PARTS), jnp.where(mode == 0, PARTS, 0))
    start = offsets[0]
    for p in (1, 2, 3):
        start = jnp.where(mode == p, offsets[3 * p], start)
    own_row = iota((DEVS, 128), 0) == me
    own_lane = iota((DEVS, 128), 1) == me
    lane8 = iota((8, 128), 1)
    bases = []
    name = jnp.zeros((DEVS, 16), jnp.int32)
    slot_lane = iota((DEVS, 16), 1).astype(F32)
    for j in range(PARTS):
        base = jnp.sum(jnp.where(own_row, offsets[j] - start, 0.0), axis=0, keepdims=True)
        inside = jnp.logical_and(j >= begin, j < end)
        base = jnp.broadcast_to(base + jnp.where(inside, 0.0, -1e6), (8, 128))
        bases.append(base + (lane8 * 16).astype(F32))
        reach = jnp.sum(jnp.where(own_lane, offsets[j + 1] - start, 0.0), axis=1, keepdims=True)
        name = name + jnp.where(reach <= slot_lane, 1, 0)
    name_ref[...] = name

    shifts = shifts_of(attempt)
    wide = jnp.where((attempt & 1) == 0, 24, 0)
    spots = []
    slot_ref[...] = jnp.zeros_like(slot_ref)
    for h in range(2):
        mine = bases[5 * h : 5 * h + 5]
        passed = (lane8 >= 64 * h) & (lane8 < 64 * h + wide)
        final = jnp.where(passed, pltpu.roll(mine[4], 96, 1), mine[3])
        rolled = [pltpu.roll(mine[0], 64, 1) if h else mine[0]]
        for k, base in ((1, mine[1]), (2, mine[2]), (3, final)):
            rolled.append(pltpu.roll(base, (128 - shifts[3 * h + k - 1]) & 127, 1))
        column = jnp.concatenate(
            [jnp.broadcast_to(base[0:1], (128, 128)).T[:, 0:1] for base in rolled], axis=0
        )
        hit = ones_where(labels_ref[h] == iota((CLUSTERS, TOK), 0)).astype(BF)
        at = dot(orders[h], hit)
        flat = jnp.sum(at * column, axis=0, keepdims=True) + within_ref[h : h + 1, :]
        flat = flat.astype(jnp.int32)
        owner, slot = flat >> 4, flat & 15
        inner = owner & 31
        spot = jnp.where(slot < 8, inner * 8 + slot, BLOCK + inner * 4 + slot - 8)
        spot = jnp.where(flat >= 0, (owner >> 5) * GROUP + spot, -1)
        slot_ref[h : h + 1, :] = spot
        spots.append(spot)
    packed = [
        jnp.concatenate([ref[:, (2 + h) * HD : (3 + h) * HD] for ref in (q_ref, k_ref, v_ref, g_ref)], axis=1)
        for h in range(2)
    ]
    rows = iota((GROUP, TOK), 0)
    copies = []
    for i in range(GROUPS):
        total = 0.0
        for h in range(2):
            pick = ones_where(rows + i * GROUP == spots[h]).astype(BF)
            total = total + dot(pick, packed[h])
        copies.append(store_group(total, i, stage, send_ref, sems))
    for copy in copies:
        copy.wait()


def store_group(total, i, stage, to_ref, sems):
    near = pl.ds(i * BLOCK, BLOCK)
    stage[near, : 4 * HD] = total[:BLOCK].astype(BF)
    stage[near, 4 * HD :] = fold(total[BLOCK:])
    copy = pltpu.make_async_copy(stage.at[near], to_ref.at[near], sems.at[i])
    copy.start()
    return copy


def attend(q, k, v, g, keep):
    scores = jnp.where(keep, dot(q, k, NT) * FACTOR, MASKED)
    raised = jnp.exp(scores - jnp.max(scores, axis=1, keepdims=True))
    weights = raised * (1.0 / jnp.sum(raised, axis=1, keepdims=True))
    rounded = weights.astype(BF)
    out = dot(rounded, v).astype(BF)
    row_dot = jnp.sum(g.astype(F32) * out.astype(F32), axis=1, keepdims=True)
    grad_score = (weights * (dot(g, v, NT) - row_dot) * FACTOR).astype(BF)
    return out, dot(grad_score, k), dot(grad_score, q, TN), dot(rounded, g, TN)


def position(index):
    group = sum(jnp.where(index >= n * GROUP, 1, 0) for n in range(1, GROUPS))
    inner = index - group * GROUP
    rest = inner - BLOCK
    near = (inner >> 3) * 16 + (inner & 7)
    far = (rest >> 2) * 16 + 8 + (rest & 3)
    return group * 512 + jnp.where(inner < BLOCK, near, far)


def routed_kernel(
    got_ref, name_col_ref, name_row_ref, out_ref, rows, gk_sum, gv_sum, stage, sems
):
    spread_out(got_ref, rows)
    copies = []
    for i in reversed(range(GROUPS)):
        here = slice(i * GROUP, (i + 1) * GROUP)
        upto = slice(0, (i + 1) * GROUP)
        same = name_col_ref[here, :] == name_row_ref[:, upto]
        past = position(iota((1, (i + 1) * GROUP), 1)) <= position(iota((GROUP, 1), 0) + i * GROUP)
        out, gq, gk, gv = attend(
            rows[here, 0:HD],
            rows[upto, HD : 2 * HD],
            rows[upto, 2 * HD : 3 * HD],
            rows[here, 3 * HD :],
            same & past,
        )
        if i == GROUPS - 1:
            gk_sum[...] = gk
            gv_sum[...] = gv
        else:
            gk_sum[upto, :] += gk
            gv_sum[upto, :] += gv
        total = jnp.concatenate([out.astype(F32), gq, gk_sum[here, :], gv_sum[here, :]], axis=1)
        copies.append(store_group(total, i, stage, out_ref, sems))
    for copy in copies:
        copy.wait()


def window_kernel(
    where_ref, q_ref, k_ref, v_ref, g_ref, halo_ref, out_ref, gq_ref, gk_ref, gv_ref, edge_ref
):
    first = where_ref[0] == 0
    row = iota((BLOCK, 2 * BLOCK), 0)
    lane = iota((BLOCK, 2 * BLOCK), 1)
    band = (lane <= row + BLOCK) & (lane >= row)
    for h in range(2):
        at = slice(h * HD, (h + 1) * HD)
        at_v = slice((2 + h) * HD, (3 + h) * HD)
        k0 = jnp.concatenate([halo_ref[:, at], k_ref[0:BLOCK, at]], axis=0)
        v0 = jnp.concatenate([halo_ref[:, at_v], v_ref[0:BLOCK, at]], axis=0)
        keep = band & (lane >= jnp.where(first, BLOCK, 0))
        out, gq, gk, gv = attend(q_ref[0:BLOCK, at], k0, v0, g_ref[0:BLOCK, at], keep)
        out_ref[0:BLOCK, at] = out
        gq_ref[0:BLOCK, at] = gq.astype(BF)
        edge_ref[:, at] = gk[0:BLOCK].astype(BF)
        edge_ref[:, at_v] = gv[0:BLOCK].astype(BF)
        out, gq, gk1, gv1 = attend(
            q_ref[BLOCK:, at], k_ref[:, at], v_ref[:, at], g_ref[BLOCK:, at], band
        )
        out_ref[BLOCK:, at] = out
        gq_ref[BLOCK:, at] = gq.astype(BF)
        gk_ref[0:BLOCK, at] = gk[BLOCK:] + gk1[0:BLOCK]
        gk_ref[BLOCK:, at] = gk1[BLOCK:]
        gv_ref[0:BLOCK, at] = gv[BLOCK:] + gv1[0:BLOCK]
        gv_ref[BLOCK:, at] = gv1[BLOCK:]


def edge_kernel(gk_l, gv_l, edge_ref, gk_ref, gv_ref):
    half = 2 * HD
    for ref, mine, edge in (
        (gk_ref, gk_l, edge_ref[:, 0:half]),
        (gv_ref, gv_l, edge_ref[:, half:]),
    ):
        ref[0 : TOK - WINDOW, 0:half] = mine[0 : TOK - WINDOW, :].astype(BF)
        ref[TOK - WINDOW :, 0:half] = (mine[TOK - WINDOW :, :] + edge.astype(F32)).astype(BF)


def fetch(slot_ref, rows_ref, h, i):
    part = slice(i * BLOCK, (i + 1) * BLOCK)
    spot = slot_ref[h : h + 1, part].astype(F32)
    spot = jnp.broadcast_to(spot, (128, BLOCK)).T[:, 0:1].astype(jnp.int32)
    pick = ones_where(iota((BLOCK, ROWS), 1) == spot).astype(BF)
    return part, dot(pick, rows_ref[...])


def finish_kernel(slot_ref, back_ref, *refs):
    outs = refs[4:8]
    rows, stage, sems = refs[8:]
    spread_out(back_ref, rows)
    copies = []
    for i in range(TOK // BLOCK):
        for h in range(2):
            part, found = fetch(slot_ref, rows, h, i)
            for n in range(4):
                stage[n, part, h * HD : (h + 1) * HD] = found[:, n * HD : (n + 1) * HD].astype(BF)
        for n in range(4):
            copy = pltpu.make_async_copy(
                stage.at[n, pl.ds(i * BLOCK, BLOCK), :],
                outs[n].at[pl.ds(i * BLOCK, BLOCK), pl.ds(2 * HD, 2 * HD)],
                sems.at[n, i],
            )
            copy.start()
            copies.append(copy)
    for copy in copies:
        copy.wait()


def add_kernel(slot_ref, back_ref, *refs):
    before, after, rows = refs[0:4], refs[4:8], refs[8]
    spread_out(back_ref, rows)
    for h in range(2):
        to = slice((2 + h) * HD, (3 + h) * HD)
        for i in range(TOK // BLOCK):
            part, found = fetch(slot_ref, rows, h, i)
            for n in range(4):
                if h == 0:
                    after[n][part, 0 : 2 * HD] = before[n][part, 0 : 2 * HD]
                more = before[n][part, to].astype(F32) + found[:, n * HD : (n + 1) * HD]
                after[n][part, to] = more.astype(BF)


def across(rows):
    blocks = rows.reshape((DEVS, 8, WIDE))
    blocks = lax.all_to_all(blocks, "seq", split_axis=0, concat_axis=0, tiled=True)
    return blocks.reshape((NEAR, WIDE))


def local(queries, keys, values, out_grad, labels):
    half = 2 * HD
    full = shape((TOK, 4 * HD))
    me = lax.axis_index("seq").astype(jnp.int32)
    sources = (queries, keys, values, out_grad)
    labels = labels.reshape(2, 1, TOK)
    last_rows = pl.BlockSpec((WINDOW, 4 * HD), lambda i: (TOK // WINDOW - 1, 0))
    tail = call(
        tail_kernel,
        shape((WINDOW, 4 * HD)),
        [last_rows] * 2,
        pl.BlockSpec((WINDOW, 4 * HD), lambda i: (0, 0)),
        moved=2**19,
        grid=(1,),
    )(keys, values)
    steps = [(s, s + 1) for s in range(DEVS - 1)]
    halo = lax.ppermute(tail, "seq", steps)
    counts, within = call(
        count_kernel,
        (shape((DEVS, 8, 128)), shape((8, TOK), F32)),
        [VMEM],
        (VMEM,) * 2,
        flops=2 * 2 * TOK**3,
        moved=2**20,
    )(labels)
    counts, halo = lax.optimization_barrier((counts, halo))
    counts = lax.all_to_all(counts, "seq", split_axis=0, concat_axis=0, tiled=True)

    def window(halo):
        return call(
            window_kernel,
            (
                full,
                full,
                shape((TOK, half), F32),
                shape((TOK, half), F32),
                shape((WINDOW, 2 * half)),
            ),
            [SMEM] + [VMEM] * 5,
            (VMEM,) * 5,
            flops=4 * 6 * 2 * 256 * 512 * 128,
            moved=6 * 2**20,
        )(me.reshape(1), *sources, halo)

    def serve(mode, halo=None):
        send, slot, name, over = call(
            place_kernel,
            (
                shape((NEAR, WIDE)),
                shape((8, TOK), jnp.int32),
                shape((DEVS, 16), jnp.int32),
                shape((8, 128), F32),
            ),
            [SMEM] + [VMEM] * 7,
            (ANY, VMEM, VMEM, VMEM),
            scratch=(
                pltpu.VMEM((DEVS * 8, 128), F32),
                pltpu.VMEM((8, DEVS, 128), F32),
                pltpu.VMEM((NEAR, WIDE), BF),
                pltpu.SemaphoreType.DMA((GROUPS,)),
            ),
            flops=2 * 2 * ROWS * TOK * TOK,
            moved=6 * 2**20,
        )(jnp.stack([me, mode]), counts, labels, within, *sources)
        mine = None
        if halo is not None:
            send, halo = lax.optimization_barrier((send, halo))
        got = across(send)
        if halo is not None:
            *mine, edge = window(halo)
            got, edge = lax.optimization_barrier((got, edge))
            edge = lax.ppermute(edge, "seq", [(b, a) for a, b in steps])
        near = name[:, :8].reshape(GROUPS, BLOCK)
        far = name[:, 8:CAP].reshape(GROUPS, GROUP - BLOCK)
        names = jnp.concatenate([near, far], axis=1)
        results = call(
            routed_kernel,
            shape((NEAR, WIDE)),
            [VMEM] * 3,
            ANY,
            scratch=(
                pltpu.VMEM((ROWS, 4 * HD), BF),
                pltpu.VMEM((ROWS, HD), F32),
                pltpu.VMEM((ROWS, HD), F32),
                pltpu.VMEM((NEAR, WIDE), BF),
                pltpu.SemaphoreType.DMA((GROUPS,)),
            ),
            flops=6 * ROWS * ROWS * HD,
            moved=4 * 2**20,
        )(got, names.reshape(ROWS, 1), names.reshape(1, ROWS))
        if halo is not None:
            results, edge = lax.optimization_barrier((results, edge))
            mine.append(edge)
        return across(results), slot, over, mine

    back, slot, over, (out_l, gq_l, gk_l, gv_l, edge) = serve(jnp.int32(0), halo)
    for distance in (1, 2):
        turn = [(x, (x + distance) % 4) for x in range(4)]
        over = jnp.maximum(over, lax.ppermute(over, "head", turn))
    gk_l, gv_l = call(
        edge_kernel, (full, full), [VMEM] * 3, (VMEM,) * 2, flops=2**20, moved=2**21
    )(gk_l, gv_l, edge)
    rows_scratch = pltpu.VMEM((ROWS, 4 * HD), BF)
    results = call(
        finish_kernel,
        (full,) * 4,
        [VMEM, VMEM] + [ANY] * 4,
        (ANY,) * 4,
        scratch=(
            rows_scratch,
            pltpu.VMEM((4, TOK, half), BF),
            pltpu.SemaphoreType.DMA((4, TOK // BLOCK)),
        ),
        flops=2 * 2 * ROWS * TOK * TOK,
        moved=6 * 2**20,
        aliases={2: 0, 3: 1, 4: 2, 5: 3},
    )(slot, back, out_l, gq_l, gk_l, gv_l)
    last = jnp.where(over[0, 0] > 0.5, 4, 1).astype(jnp.int32)

    def again(mode, sums):
        more, spot, _, _ = serve(mode)
        return call(
            add_kernel, (full,) * 4, [VMEM] * 6, (VMEM,) * 4, scratch=(rows_scratch,)
        )(spot, more, *sums)

    return lax.fori_loop(1, last, again, results)


def solution(mesh):
    spec = P("seq", "head")
    return jax.shard_map(
        local,
        mesh=mesh,
        in_specs=(spec, spec, spec, spec, P("head", "seq", None)),
        out_specs=(spec, spec, spec, spec),
        check_vma=False,
    )
```

time: 561 us -> 244 us (0.43)
  the two profiles are of different devices: /device:TPU:127 before, /device:TPU:39 now
where the time goes in v1:
time: 244 us
  waiting for transfers between devices  165 us (68%)
  starting transfers between devices  46.1 us (19%)
  Pallas kernels  29.8 us (12%)
    all_to_all x2, waiting for transfers between devices, across(): lax.all_to_all(blocks, 'seq', split_axis=0, concat_axis=0, tiled=True)  135 us
    all_to_all x1, waiting for transfers between devices, local(): lax.all_to_all(counts, 'seq', split_axis=0, concat_axis=0, tiled=True)  22.1 us
    all_to_all x1, starting transfers between devices, local(): lax.all_to_all(counts, 'seq', split_axis=0, concat_axis=0, tiled=True)  21.3 us
    all_to_all x2, starting transfers between devices, across(): lax.all_to_all(blocks, 'seq', split_axis=0, concat_axis=0, tiled=True)  14.6 us
    pallas_call x1, Pallas kernels, serve(): call(routed_kernel, shape((NEAR, WIDE)), [VMEM] * 3, ANY, scratch=(pltpu....  8.66 us
    pallas_call x1, Pallas kernels, serve(): call(place_kernel, (shape((NEAR, WIDE)), shape((8, TOK), jnp.int32), shap...  7.02 us
    ppermute x2, waiting for transfers between devices, local(): over = jnp.maximum(over, lax.ppermute(over, 'head', turn))  6.53 us
    pallas_call x1, Pallas kernels, window(): call(window_kernel, (full, full, shape((TOK, half), F32), shape((TOK, hal...  5.79 us
  transfers between devices with their start and end apart: 7, of which 6 were waited for; matrix products, arithmetic and copies ran while one was open for 0% of the time, Pallas kernels for 8%

profile of v1, /device:TPU:39, one launch (start us, length us, event | category | flops | bytes accessed | tf_op | source)
XLA Modules:
  0.0 243.7 jit_solution(4302482383779325024)
XLA Ops:
  0.6 1.1 shard_map.85
  1.7 0.0 copy-start.1
  1.7 3.8 %collective-permute-start = (bf16[256,512]{1,0:T(8,128)(2,1)S(1)}, bf16[256,512]{1,0:T(8,128)(2,1)S(1)}, u32[]{:S(2)}, u32[]{:S(2)}) collective-permute-start(bf16[256,512]{1,0:T(8,128)(2,1)S(1)} %shard_map.85), channel_id=1, source_target_pairs={{0,4},{4,8},{8,12},{12,16},{16,20},{20,24},{24,28},{28,32},{32,36}... | collective-permute-start | bytes 786440 | tf_op jit(solution)/shard_map/ppermute | solution.py:412
  5.5 2.2 shard_map.84
  7.7 1.1 collective-permute-done.halo_ref
  8.8 21.3 %all-to-all-start.2 = ((bf16[128,8,128]{2,1,0:T(8,128)(2,1)}), bf16[128,8,128]{2,1,0:T(8,128)(2,1)}, u32[]{:S(2)}, u32[]{:S(2)}) async-start(bf16[128,8,128]{2,1,0:T(8,128)(2,1)} %get-tuple-element.113), calls=%async_computation.2 | async-start | bytes 524288 | tf_op jit(solution)/shard_map/all_to_all | solution.py:422
  30.0 0.1 pad_add_fusion.1.where_ref
  30.1 22.1 %all-to-all-done.2.counts_ref = bf16[128,8,128]{2,1,0:T(8,128)(2,1)} async-done(((bf16[128,8,128]{2,1,0:T(8,128)(2,1)}), bf16[128,8,128]{2,1,0:T(8,128)(2,1)}, u32[]{:S(2)}, u32[]{:S(2)}) %all-to-all-start.2) | async-done | bytes 262176 | tf_op jit(solution)/shard_map/all_to_all | solution.py:422
  52.2 0.0 copy-done.1
  52.2 7.0 %shard_map.86 = (bf16[1024,768]{1,0:T(8,128)(2,1)}, s32[8,512]{1,0:T(8,128)S(1)}, s32[128,16]{1,0:T(8,128)S(1)}, f32[8,128]{1,0:T(8,128)S(1)}) custom-call(s32[2]{0:T(128)S(1)} %pad_add_fusion.1.where_ref, bf16[128,8,128]{2,1,0:T(8,128)(2,1)} %all-to-all-done.2.counts_ref, s32[2,1,512]{2,1,0:T(1,128)S(1)} %bitcast.64, ...), custom_call_target="tpu_custom_call" | custom-call | flops 1610612736 | bytes 6291456 | tf_op jit(solution)/shard_map/pallas_call | solution.py:441
  59.3 6.2 %all-to-all-start.3 = ((bf16[128,8,768]{2,1,0:T(8,128)(2,1)}), bf16[128,8,768]{2,1,0:T(8,128)(2,1)S(1)}, u32[]{:S(2)}, u32[]{:S(2)}) async-start(bf16[128,8,768]{2,1,0:T(8,128)(2,1)} %bitcast.8), calls=%async_computation.3 | async-start | bytes 3145728 | tf_op jit(solution)/shard_map/all_to_all | solution.py:392
  65.5 0.1 slice.16
  65.6 0.1 reshape.68
  65.7 0.1 reshape.69
  65.8 5.8 %shard_map.87 = (bf16[512,512]{1,0:T(8,128)(2,1)}, bf16[512,512]{1,0:T(8,128)(2,1)}, f32[512,256]{1,0:T(8,128)S(1)}, f32[512,256]{1,0:T(8,128)S(1)}, bf16[256,512]{1,0:T(8,128)(2,1)}) custom-call(s32[1]{0:T(128)} %bitcast.6.where_ref, bf16[512,512]{1,0:T(8,128)(2,1)} %q_ref.3, bf16[512,512]{1,0:T(8,128)(2,1)} %k_ref.5, bf16[512,512]{1,0:T(8,128)(2,1)} %v_ref.5, ...), custom_call_target="tpu_custom_call" | custom-call | flops 805306368 | bytes 6291456 | tf_op jit(solution)/shard_map/pallas_call | solution.py:425
  71.6 71.4 %all-to-all-done.3 = bf16[128,8,768]{2,1,0:T(8,128)(2,1)S(1)} async-done(((bf16[128,8,768]{2,1,0:T(8,128)(2,1)}), bf16[128,8,768]{2,1,0:T(8,128)(2,1)S(1)}, u32[]{:S(2)}, u32[]{:S(2)}) %all-to-all-start.3) | async-done | bytes 1572896 | tf_op jit(solution)/shard_map/all_to_all | solution.py:392
  143.0 2.2 collective-permute-start.1
  145.3 0.3 copy.19
  145.6 8.7 %shard_map.88 = bf16[1024,768]{1,0:T(8,128)(2,1)} custom-call(bf16[1024,768]{1,0:T(8,128)(2,1)S(1)} %bitcast.54, s32[1536,1]{1,0:T(8,128)S(1)} %bitcast.55, s32[1,1536]{1,0:T(1,128)S(1)} %bitcast.60), custom_call_target="tpu_custom_call" | custom-call | flops 1811939328 | bytes 4194304 | tf_op jit(solution)/shard_map/pallas_call | solution.py:471
  154.2 0.0 collective-permute-done.1.edge_ref
  154.3 8.4 %all-to-all-start.4 = ((bf16[128,8,768]{2,1,0:T(8,128)(2,1)}), bf16[128,8,768]{2,1,0:T(8,128)(2,1)S(1)}, u32[]{:S(2)}, u32[]{:S(2)}) async-start(bf16[128,8,768]{2,1,0:T(8,128)(2,1)} %bitcast.10), calls=%async_computation.4 | async-start | bytes 3145728 | tf_op jit(solution)/shard_map/all_to_all | solution.py:392
  162.7 1.9 collective-permute-start.2
  164.6 2.7 %collective-permute-done.2 = f32[8,128]{1,0:T(8,128)S(1)} collective-permute-done((f32[8,128]{1,0:T(8,128)S(1)}, f32[8,128]{1,0:T(8,128)S(1)}, u32[]{:S(2)}, u32[]{:S(2)}) %collective-permute-start.2) | collective-permute-done | bytes 4128 | tf_op jit(solution)/shard_map/ppermute | solution.py:494
  167.3 2.3 collective-permute-start.3
  169.7 3.8 %collective-permute-done.3 = f32[8,128]{1,0:T(8,128)S(1)} collective-permute-done((f32[8,128]{1,0:T(8,128)S(1)}, f32[8,128]{1,0:T(8,128)S(1)}, u32[]{:S(2)}, u32[]{:S(2)}) %collective-permute-start.3) | collective-permute-done | bytes 4128 | tf_op jit(solution)/shard_map/ppermute | solution.py:494
  173.5 0.5 slice.17
  174.6 2.0 shard_map.89
  176.6 63.6 %all-to-all-done.4 = bf16[128,8,768]{2,1,0:T(8,128)(2,1)S(1)} async-done(((bf16[128,8,768]{2,1,0:T(8,128)(2,1)}), bf16[128,8,768]{2,1,0:T(8,128)(2,1)S(1)}, u32[]{:S(2)}, u32[]{:S(2)}) %all-to-all-start.4) | async-done | bytes 1572896 | tf_op jit(solution)/shard_map/all_to_all | solution.py:392
  240.2 3.1 %shard_map.90 = (bf16[512,512]{1,0:T(8,128)(2,1)}, bf16[512,512]{1,0:T(8,128)(2,1)}, bf16[512,512]{1,0:T(8,128)(2,1)}, bf16[512,512]{1,0:T(8,128)(2,1)}) custom-call(s32[8,512]{1,0:T(8,128)S(1)} %get-tuple-element.115.slot_ref, bf16[1024,768]{1,0:T(8,128)(2,1)S(1)} %bitcast.53, ...), custom_call_target="tpu_custom_call", output_to_operand_aliasing={{0}: (2, {}), {1}: (3, {}), {2}: (4, {}), {3}: (5, {})} | custom-call | flops 1610612736 | bytes 6291456 | tf_op jit(solution)/shard_map/pallas_call | solution.py:499
  243.3 0.2 while.16
  (5 shorter events, 0.0 us)
Async XLA Ops:
  1.7 50.6 %copy-start.1 = (s32[2,512,1]{1,2,0:T(1,128)S(1)}, s32[2,512,1]{1,2,0:T(1,128)}, u32[]{:S(2)}) copy-start(s32[2,512,1]{1,2,0:T(1,128)} %param.11) | copy-start | bytes 12292
  1.7 7.1 %collective-permute-start = (bf16[256,512]{1,0:T(8,128)(2,1)S(1)}, bf16[256,512]{1,0:T(8,128)(2,1)S(1)}, u32[]{:S(2)}, u32[]{:S(2)}) collective-permute-start(bf16[256,512]{1,0:T(8,128)(2,1)S(1)} %shard_map.85), channel_id=1, source_target_pairs={{0,4},{4,8},{8,12},{12,16},{16,20},{20,24},{24,28},{28,32},{32,36}... | collective-permute-start | bytes 786440 | tf_op jit(solution)/shard_map/ppermute | solution.py:412
  8.8 43.5 %all-to-all-start.2 = ((bf16[128,8,128]{2,1,0:T(8,128)(2,1)}), bf16[128,8,128]{2,1,0:T(8,128)(2,1)}, u32[]{:S(2)}, u32[]{:S(2)}) async-start(bf16[128,8,128]{2,1,0:T(8,128)(2,1)} %get-tuple-element.113), calls=%async_computation.2 | async-start | bytes 524288 | tf_op jit(solution)/shard_map/all_to_all | solution.py:422
  59.3 83.8 %all-to-all-start.3 = ((bf16[128,8,768]{2,1,0:T(8,128)(2,1)}), bf16[128,8,768]{2,1,0:T(8,128)(2,1)S(1)}, u32[]{:S(2)}, u32[]{:S(2)}) async-start(bf16[128,8,768]{2,1,0:T(8,128)(2,1)} %bitcast.8), calls=%async_computation.3 | async-start | bytes 3145728 | tf_op jit(solution)/shard_map/all_to_all | solution.py:392
  143.0 11.2 %collective-permute-start.1 = (bf16[256,512]{1,0:T(8,128)(2,1)}, bf16[256,512]{1,0:T(8,128)(2,1)}, u32[]{:S(2)}, u32[]{:S(2)}) collective-permute-start(bf16[256,512]{1,0:T(8,128)(2,1)} %get-tuple-element.123), channel_id=1, source_target_pairs={{4,0},{8,4},{12,8},{16,12},{20,16},{24,20},{28,24},{32,28},{36,32}... | collective-permute-start | bytes 786440 | tf_op jit(solution)/shard_map/ppermute | solution.py:467
  154.3 86.0 %all-to-all-start.4 = ((bf16[128,8,768]{2,1,0:T(8,128)(2,1)}), bf16[128,8,768]{2,1,0:T(8,128)(2,1)S(1)}, u32[]{:S(2)}, u32[]{:S(2)}) async-start(bf16[128,8,768]{2,1,0:T(8,128)(2,1)} %bitcast.10), calls=%async_computation.4 | async-start | bytes 3145728 | tf_op jit(solution)/shard_map/all_to_all | solution.py:392
  162.7 4.6 %collective-permute-start.2 = (f32[8,128]{1,0:T(8,128)S(1)}, f32[8,128]{1,0:T(8,128)S(1)}, u32[]{:S(2)}, u32[]{:S(2)}) collective-permute-start(f32[8,128]{1,0:T(8,128)S(1)} %get-tuple-element.136), channel_id=1, source_target_pairs={{0,1},{1,2},{2,3},{3,0},{4,5},{5,6},{6,7},{7,4},{8,9},{9,10},{10,1... | collective-permute-start | bytes 12296 | tf_op jit(solution)/shard_map/ppermute | solution.py:494
  167.3 6.1 %collective-permute-start.3 = (f32[8,128]{1,0:T(8,128)S(1)}, f32[8,128]{1,0:T(8,128)S(1)}, u32[]{:S(2)}, u32[]{:S(2)}) collective-permute-start(f32[8,128]{1,0:T(8,128)S(1)} %max.6), channel_id=1, source_target_pairs={{0,2},{1,3},{2,0},{3,1},{4,6},{5,7},{6,4},{7,5},{8,10},{9,11},{10,... | collective-permute-start | bytes 12296 | tf_op jit(solution)/shard_map/ppermute | solution.py:494

commit v2 on v1

--- a/solution.py
+++ b/solution.py
@@ -418,8 +418,8 @@
         flops=2 * 2 * TOK**3,
         moved=2**20,
     )(labels)
+    counts = lax.all_to_all(counts, "seq", split_axis=0, concat_axis=0, tiled=True)
     counts, halo = lax.optimization_barrier((counts, halo))
-    counts = lax.all_to_all(counts, "seq", split_axis=0, concat_axis=0, tiled=True)
 
     def window(halo):
         return call(
@@ -463,8 +463,8 @@
         got = across(send)
         if halo is not None:
             *mine, edge = window(halo)
+            edge = lax.ppermute(edge, "seq", [(b, a) for a, b in steps])
             got, edge = lax.optimization_barrier((got, edge))
-            edge = lax.ppermute(edge, "seq", [(b, a) for a, b in steps])
         near = name[:, :8].reshape(GROUPS, BLOCK)
         far = name[:, 8:CAP].reshape(GROUPS, GROUP - BLOCK)
         names = jnp.concatenate([near, far], axis=1)
@@ -484,7 +484,6 @@
             moved=4 * 2**20,
         )(got, names.reshape(ROWS, 1), names.reshape(1, ROWS))
         if halo is not None:
-            results, edge = lax.optimization_barrier((results, edge))
             mine.append(edge)
         return across(results), slot, over, mine
 

time: 244 us -> 236 us (0.967)
  waiting for transfers between devices: 165 us -> 156 us
    all_to_all x2, waiting for transfers between devices: 135 us -> 126 us  [across(): lax.all_to_all(blocks, 'seq', split_axis=0, concat_axis=0, tiled=True)]
    all_to_all x1, waiting for transfers between devices: 22.1 us -> 13.9 us  [local(): lax.all_to_all(counts, 'seq', split_axis=0, concat_axis=0, tiled=True)]
    ppermute x1, waiting for transfers between devices: 0.01 us -> 6.07 us  [serve(): edge = lax.ppermute(edge, 'seq', [(b, a) for a, b in steps])]
    ppermute x1, waiting for transfers between devices: 1.1 us -> 3.85 us  [local(): halo = lax.ppermute(tail, 'seq', steps)]
  transfers between devices with their start and end apart: 7 -> 7, of which waited for: 6 -> 7; matrix products, arithmetic and copies ran while one was open for 0% -> 1% of each run, Pallas kernels for 8% -> 4%
where the time goes in v2:
time: 236 us
  waiting for transfers between devices  156 us (66%)
  starting transfers between devices  47.9 us (20%)
  Pallas kernels  29.1 us (12%)
    all_to_all x2, waiting for transfers between devices, across(): lax.all_to_all(blocks, 'seq', split_axis=0, concat_axis=0, tiled=True)  126 us
    all_to_all x1, starting transfers between devices, local(): lax.all_to_all(counts, 'seq', split_axis=0, concat_axis=0, tiled=True)  19.9 us
    all_to_all x2, starting transfers between devices, across(): lax.all_to_all(blocks, 'seq', split_axis=0, concat_axis=0, tiled=True)  17 us
    all_to_all x1, waiting for transfers between devices, local(): lax.all_to_all(counts, 'seq', split_axis=0, concat_axis=0, tiled=True)  13.9 us
    pallas_call x1, Pallas kernels, serve(): call(routed_kernel, shape((NEAR, WIDE)), [VMEM] * 3, ANY, scratch=(pltpu....  8.66 us
    pallas_call x1, Pallas kernels, serve(): call(place_kernel, (shape((NEAR, WIDE)), shape((8, TOK), jnp.int32), shap...  6.32 us
    ppermute x1, waiting for transfers between devices, serve(): edge = lax.ppermute(edge, 'seq', [(b, a) for a, b in steps])  6.07 us
    pallas_call x1, Pallas kernels, window(): call(window_kernel, (full, full, shape((TOK, half), F32), shape((TOK, hal...  5.8 us
  transfers between devices with their start and end apart: 7, of which 7 were waited for; matrix products, arithmetic and copies ran while one was open for 1% of the time, Pallas kernels for 4%

profile of v2, /device:TPU:39, one launch (start us, length us, event | category | flops | bytes accessed | tf_op | source)
XLA Modules:
  0.0 235.6 jit_solution(17259167238717100651)
XLA Ops:
  0.6 0.0 copy-start.1
  0.6 2.3 shard_map.84
  2.9 19.9 %all-to-all-start.2 = ((bf16[128,8,128]{2,1,0:T(8,128)(2,1)}), bf16[128,8,128]{2,1,0:T(8,128)(2,1)}, u32[]{:S(2)}, u32[]{:S(2)}) async-start(bf16[128,8,128]{2,1,0:T(8,128)(2,1)} %get-tuple-element.110), calls=%async_computation.2 | async-start | bytes 524288 | tf_op jit(solution)/shard_map/all_to_all | solution.py:421
  22.8 1.1 shard_map.85
  23.9 3.3 %collective-permute-start = (bf16[256,512]{1,0:T(8,128)(2,1)S(1)}, bf16[256,512]{1,0:T(8,128)(2,1)S(1)}, u32[]{:S(2)}, u32[]{:S(2)}) collective-permute-start(bf16[256,512]{1,0:T(8,128)(2,1)S(1)} %shard_map.85), channel_id=1, source_target_pairs={{0,4},{4,8},{8,12},{12,16},{16,20},{20,24},{24,28},{28,32},{32,36}... | collective-permute-start | bytes 786440 | tf_op jit(solution)/shard_map/ppermute | solution.py:412
  27.2 0.1 pad_add_fusion.1.where_ref
  27.3 3.9 %collective-permute-done.halo_ref = bf16[256,512]{1,0:T(8,128)(2,1)S(1)} collective-permute-done((bf16[256,512]{1,0:T(8,128)(2,1)S(1)}, bf16[256,512]{1,0:T(8,128)(2,1)S(1)}, u32[]{:S(2)}, u32[]{:S(2)}) %collective-permute-start) | collective-permute-done | bytes 262176 | tf_op jit(solution)/shard_map/ppermute | solution.py:412
  31.2 13.9 %all-to-all-done.2.counts_ref = bf16[128,8,128]{2,1,0:T(8,128)(2,1)} async-done(((bf16[128,8,128]{2,1,0:T(8,128)(2,1)}), bf16[128,8,128]{2,1,0:T(8,128)(2,1)}, u32[]{:S(2)}, u32[]{:S(2)}) %all-to-all-start.2) | async-done | bytes 262176 | tf_op jit(solution)/shard_map/all_to_all | solution.py:421
  45.1 0.0 copy-done.1
  45.1 6.3 %shard_map.86 = (bf16[1024,768]{1,0:T(8,128)(2,1)}, s32[8,512]{1,0:T(8,128)S(1)}, s32[128,16]{1,0:T(8,128)S(1)}, f32[8,128]{1,0:T(8,128)S(1)}) custom-call(s32[2]{0:T(128)S(1)} %pad_add_fusion.1.where_ref, bf16[128,8,128]{2,1,0:T(8,128)(2,1)} %all-to-all-done.2.counts_ref, s32[2,1,512]{2,1,0:T(1,128)S(1)} %bitcast.64, ...), custom_call_target="tpu_custom_call" | custom-call | flops 1610612736 | bytes 6291456 | tf_op jit(solution)/shard_map/pallas_call | solution.py:441
  51.4 8.0 %all-to-all-start.3 = ((bf16[128,8,768]{2,1,0:T(8,128)(2,1)}), bf16[128,8,768]{2,1,0:T(8,128)(2,1)S(1)}, u32[]{:S(2)}, u32[]{:S(2)}) async-start(bf16[128,8,768]{2,1,0:T(8,128)(2,1)} %bitcast.8), calls=%async_computation.3 | async-start | bytes 3145728 | tf_op jit(solution)/shard_map/all_to_all | solution.py:392
  59.4 5.8 %shard_map.87 = (bf16[512,512]{1,0:T(8,128)(2,1)}, bf16[512,512]{1,0:T(8,128)(2,1)}, f32[512,256]{1,0:T(8,128)S(1)}, f32[512,256]{1,0:T(8,128)S(1)}, bf16[256,512]{1,0:T(8,128)(2,1)}) custom-call(s32[1]{0:T(128)} %bitcast.6.where_ref, bf16[512,512]{1,0:T(8,128)(2,1)} %q_ref.3, bf16[512,512]{1,0:T(8,128)(2,1)} %k_ref.5, bf16[512,512]{1,0:T(8,128)(2,1)} %v_ref.5, ...), custom_call_target="tpu_custom_call" | custom-call | flops 805306368 | bytes 6291456 | tf_op jit(solution)/shard_map/pallas_call | solution.py:425
  65.2 2.5 %collective-permute-start.1 = (bf16[256,512]{1,0:T(8,128)(2,1)}, bf16[256,512]{1,0:T(8,128)(2,1)}, u32[]{:S(2)}, u32[]{:S(2)}) collective-permute-start(bf16[256,512]{1,0:T(8,128)(2,1)} %get-tuple-element.118), channel_id=1, source_target_pairs={{4,0},{8,4},{12,8},{16,12},{20,16},{24,20},{28,24},{32,28},{36,32}... | collective-permute-start | bytes 786440 | tf_op jit(solution)/shard_map/ppermute | solution.py:466
  67.8 0.1 slice.16
  67.8 0.1 reshape.69
  67.9 0.1 reshape.68
  68.1 0.3 copy.19
  68.4 6.1 %collective-permute-done.1.edge_ref = bf16[256,512]{1,0:T(8,128)(2,1)} collective-permute-done((bf16[256,512]{1,0:T(8,128)(2,1)}, bf16[256,512]{1,0:T(8,128)(2,1)}, u32[]{:S(2)}, u32[]{:S(2)}) %collective-permute-start.1) | collective-permute-done | bytes 262176 | tf_op jit(solution)/shard_map/ppermute | solution.py:466
  74.5 62.5 %all-to-all-done.3 = bf16[128,8,768]{2,1,0:T(8,128)(2,1)S(1)} async-done(((bf16[128,8,768]{2,1,0:T(8,128)(2,1)}), bf16[128,8,768]{2,1,0:T(8,128)(2,1)S(1)}, u32[]{:S(2)}, u32[]{:S(2)}) %all-to-all-start.3) | async-done | bytes 1572896 | tf_op jit(solution)/shard_map/all_to_all | solution.py:392
  136.9 8.7 %shard_map.88 = bf16[1024,768]{1,0:T(8,128)(2,1)} custom-call(bf16[1024,768]{1,0:T(8,128)(2,1)S(1)} %bitcast.54, s32[1536,1]{1,0:T(8,128)S(1)} %bitcast.55, s32[1,1536]{1,0:T(1,128)S(1)} %bitcast.60), custom_call_target="tpu_custom_call" | custom-call | flops 1811939328 | bytes 4194304 | tf_op jit(solution)/shard_map/pallas_call | solution.py:471
  145.6 9.0 %all-to-all-start.4 = ((bf16[128,8,768]{2,1,0:T(8,128)(2,1)}), bf16[128,8,768]{2,1,0:T(8,128)(2,1)S(1)}, u32[]{:S(2)}, u32[]{:S(2)}) async-start(bf16[128,8,768]{2,1,0:T(8,128)(2,1)} %bitcast.10), calls=%async_computation.4 | async-start | bytes 3145728 | tf_op jit(solution)/shard_map/all_to_all | solution.py:392
  154.6 2.1 collective-permute-start.2
  156.7 2.5 %collective-permute-done.2 = f32[8,128]{1,0:T(8,128)S(1)} collective-permute-done((f32[8,128]{1,0:T(8,128)S(1)}, f32[8,128]{1,0:T(8,128)S(1)}, u32[]{:S(2)}, u32[]{:S(2)}) %collective-permute-start.2) | collective-permute-done | bytes 4128 | tf_op jit(solution)/shard_map/ppermute | solution.py:493
  159.2 3.0 %collective-permute-start.3 = (f32[8,128]{1,0:T(8,128)S(1)}, f32[8,128]{1,0:T(8,128)S(1)}, u32[]{:S(2)}, u32[]{:S(2)}) collective-permute-start(f32[8,128]{1,0:T(8,128)S(1)} %max.6), channel_id=1, source_target_pairs={{0,2},{1,3},{2,0},{3,1},{4,6},{5,7},{6,4},{7,5},{8,10},{9,11},{10,... | collective-permute-start | bytes 12296 | tf_op jit(solution)/shard_map/ppermute | solution.py:493
  162.2 3.1 %collective-permute-done.3 = f32[8,128]{1,0:T(8,128)S(1)} collective-permute-done((f32[8,128]{1,0:T(8,128)S(1)}, f32[8,128]{1,0:T(8,128)S(1)}, u32[]{:S(2)}, u32[]{:S(2)}) %collective-permute-start.3) | collective-permute-done | bytes 4128 | tf_op jit(solution)/shard_map/ppermute | solution.py:493
  165.4 0.5 slice.17
  166.5 2.0 shard_map.89
  168.5 63.6 %all-to-all-done.4 = bf16[128,8,768]{2,1,0:T(8,128)(2,1)S(1)} async-done(((bf16[128,8,768]{2,1,0:T(8,128)(2,1)}), bf16[128,8,768]{2,1,0:T(8,128)(2,1)S(1)}, u32[]{:S(2)}, u32[]{:S(2)}) %all-to-all-start.4) | async-done | bytes 1572896 | tf_op jit(solution)/shard_map/all_to_all | solution.py:392
  232.1 3.1 %shard_map.90 = (bf16[512,512]{1,0:T(8,128)(2,1)}, bf16[512,512]{1,0:T(8,128)(2,1)}, bf16[512,512]{1,0:T(8,128)(2,1)}, bf16[512,512]{1,0:T(8,128)(2,1)}) custom-call(s32[8,512]{1,0:T(8,128)S(1)} %get-tuple-element.113.slot_ref, bf16[1024,768]{1,0:T(8,128)(2,1)S(1)} %bitcast.53, ...), custom_call_target="tpu_custom_call", output_to_operand_aliasing={{0}: (2, {}), {1}: (3, {}), {2}: (4, {}), {3}: (5, {})} | custom-call | flops 1610612736 | bytes 6291456 | tf_op jit(solution)/shard_map/pallas_call | solution.py:498
  235.2 0.2 while.16
  (5 shorter events, 0.0 us)
Async XLA Ops:
  0.6 44.4 %copy-start.1 = (s32[2,512,1]{1,2,0:T(1,128)S(1)}, s32[2,512,1]{1,2,0:T(1,128)}, u32[]{:S(2)}) copy-start(s32[2,512,1]{1,2,0:T(1,128)} %param.11) | copy-start | bytes 12292
  2.9 42.2 %all-to-all-start.2 = ((bf16[128,8,128]{2,1,0:T(8,128)(2,1)}), bf16[128,8,128]{2,1,0:T(8,128)(2,1)}, u32[]{:S(2)}, u32[]{:S(2)}) async-start(bf16[128,8,128]{2,1,0:T(8,128)(2,1)} %get-tuple-element.110), calls=%async_computation.2 | async-start | bytes 524288 | tf_op jit(solution)/shard_map/all_to_all | solution.py:421
  23.9 7.3 %collective-permute-start = (bf16[256,512]{1,0:T(8,128)(2,1)S(1)}, bf16[256,512]{1,0:T(8,128)(2,1)S(1)}, u32[]{:S(2)}, u32[]{:S(2)}) collective-permute-start(bf16[256,512]{1,0:T(8,128)(2,1)S(1)} %shard_map.85), channel_id=1, source_target_pairs={{0,4},{4,8},{8,12},{12,16},{16,20},{20,24},{24,28},{28,32},{32,36}... | collective-permute-start | bytes 786440 | tf_op jit(solution)/shard_map/ppermute | solution.py:412
  51.4 85.5 %all-to-all-start.3 = ((bf16[128,8,768]{2,1,0:T(8,128)(2,1)}), bf16[128,8,768]{2,1,0:T(8,128)(2,1)S(1)}, u32[]{:S(2)}, u32[]{:S(2)}) async-start(bf16[128,8,768]{2,1,0:T(8,128)(2,1)} %bitcast.8), calls=%async_computation.3 | async-start | bytes 3145728 | tf_op jit(solution)/shard_map/all_to_all | solution.py:392
  65.2 9.3 %collective-permute-start.1 = (bf16[256,512]{1,0:T(8,128)(2,1)}, bf16[256,512]{1,0:T(8,128)(2,1)}, u32[]{:S(2)}, u32[]{:S(2)}) collective-permute-start(bf16[256,512]{1,0:T(8,128)(2,1)} %get-tuple-element.118), channel_id=1, source_target_pairs={{4,0},{8,4},{12,8},{16,12},{20,16},{24,20},{28,24},{32,28},{36,32}... | collective-permute-start | bytes 786440 | tf_op jit(solution)/shard_map/ppermute | solution.py:466
  145.6 86.5 %all-to-all-start.4 = ((bf16[128,8,768]{2,1,0:T(8,128)(2,1)}), bf16[128,8,768]{2,1,0:T(8,128)(2,1)S(1)}, u32[]{:S(2)}, u32[]{:S(2)}) async-start(bf16[128,8,768]{2,1,0:T(8,128)(2,1)} %bitcast.10), calls=%async_computation.4 | async-start | bytes 3145728 | tf_op jit(solution)/shard_map/all_to_all | solution.py:392
  154.6 4.6 %collective-permute-start.2 = (f32[8,128]{1,0:T(8,128)S(1)}, f32[8,128]{1,0:T(8,128)S(1)}, u32[]{:S(2)}, u32[]{:S(2)}) collective-permute-start(f32[8,128]{1,0:T(8,128)S(1)} %get-tuple-element.132), channel_id=1, source_target_pairs={{0,1},{1,2},{2,3},{3,0},{4,5},{5,6},{6,7},{7,4},{8,9},{9,10},{10,1... | collective-permute-start | bytes 12296 | tf_op jit(solution)/shard_map/ppermute | solution.py:493
  159.2 6.1 %collective-permute-start.3 = (f32[8,128]{1,0:T(8,128)S(1)}, f32[8,128]{1,0:T(8,128)S(1)}, u32[]{:S(2)}, u32[]{:S(2)}) collective-permute-start(f32[8,128]{1,0:T(8,128)S(1)} %max.6), channel_id=1, source_target_pairs={{0,2},{1,3},{2,0},{3,1},{4,6},{5,7},{6,4},{7,5},{8,10},{9,11},{10,... | collective-permute-start | bytes 12296 | tf_op jit(solution)/shard_map/ppermute | solution.py:493

commit v3 on v2

--- a/solution.py
+++ b/solution.py
@@ -20,6 +20,7 @@
 ROWS = GROUP * GROUPS
 PARTS = 10
 TRIES = 64
+GAP = 40
 TURNS = ((37, 11), (59, 77), (83, 40), (101, 95), (29, 23), (71, 118))
 BLOCK = 256
 MASKED = -1e30
@@ -105,18 +106,26 @@
     tail_ref[:, half:] = v_ref[:, :half]
 
 
-def count_kernel(labels_ref, counts_ref, within_ref):
-    later = ones_where(iota((TOK, TOK), 0) < iota((TOK, TOK), 1)).astype(BF)
+def hits(labels_ref, h):
+    return ones_where(labels_ref[h] == iota((CLUSTERS, TOK), 0)).astype(BF)
+
+
+def count_kernel(labels_ref, counts_ref):
     rows = []
-    within_ref[...] = jnp.zeros_like(within_ref)
-    for h in range(2):
-        hit = ones_where(labels_ref[h] == iota((CLUSTERS, TOK), 0))
-        total = dot(jnp.ones((8, TOK), BF), hit.astype(BF), NT)
+    for h in range(2):
+        total = dot(jnp.ones((8, TOK), BF), hits(labels_ref, h), NT)
         rows += [total[0:1, k * 128 : (k + 1) * 128] for k in range(4)]
-        before = dot(hit.astype(BF), later)
-        within_ref[h : h + 1, :] = jnp.sum(hit * before, axis=0, keepdims=True)
     table = jnp.concatenate(rows, axis=0)
     counts_ref[...] = jnp.broadcast_to(table[None], (DEVS, 8, 128)).astype(BF)
+
+
+def rank_kernel(labels_ref, within_ref):
+    later = ones_where(iota((TOK, TOK), 0) < iota((TOK, TOK), 1)).astype(BF)
+    within_ref[...] = jnp.zeros_like(within_ref)
+    for h in range(2):
+        hit = hits(labels_ref, h)
+        before = dot(hit, later) * hit.astype(F32)
+        within_ref[h : h + 1, :] = jnp.sum(before, axis=0, keepdims=True)
 
 
 def shifts_of(attempt):
@@ -134,7 +143,7 @@
         final = pltpu.roll(ranked[4 * h + 3], shifts[3 * h + 2], 1)
         passed = (lane >= 64 * h) & (lane < 64 * h + wide)
         lists.append(jnp.where(passed, 0.0, final))
-        lists.append(pltpu.roll(jnp.where(passed, final, 0.0), 32, 1))
+        lists.append(pltpu.roll(jnp.where(passed, final, 0.0), GAP, 1))
     return lists
 
 
@@ -213,7 +222,7 @@
     for h in range(2):
         mine = bases[5 * h : 5 * h + 5]
         passed = (lane8 >= 64 * h) & (lane8 < 64 * h + wide)
-        final = jnp.where(passed, pltpu.roll(mine[4], 96, 1), mine[3])
+        final = jnp.where(passed, pltpu.roll(mine[4], 128 - GAP, 1), mine[3])
         rolled = [pltpu.roll(mine[0], 64, 1) if h else mine[0]]
         for k, base in ((1, mine[1]), (2, mine[2]), (3, final)):
             rolled.append(pltpu.roll(base, (128 - shifts[3 * h + k - 1]) & 127, 1))
@@ -256,23 +265,22 @@
 
 
 def attend(q, k, v, g, keep):
-    scores = jnp.where(keep, dot(q, k, NT) * FACTOR, MASKED)
-    raised = jnp.exp(scores - jnp.max(scores, axis=1, keepdims=True))
+    scores = jnp.where(keep, dot(q, k, NT) * (FACTOR * math.log2(math.e)), MASKED)
+    raised = jnp.exp2(scores - jnp.max(scores, axis=1, keepdims=True))
     weights = raised * (1.0 / jnp.sum(raised, axis=1, keepdims=True))
     rounded = weights.astype(BF)
     out = dot(rounded, v).astype(BF)
     row_dot = jnp.sum(g.astype(F32) * out.astype(F32), axis=1, keepdims=True)
-    grad_score = (weights * (dot(g, v, NT) - row_dot) * FACTOR).astype(BF)
-    return out, dot(grad_score, k), dot(grad_score, q, TN), dot(rounded, g, TN)
+    grad_score = (weights * (dot(g, v, NT) - row_dot)).astype(BF)
+    grad_k = dot(q, grad_score, TN).T * FACTOR
+    return out, dot(grad_score, k) * FACTOR, grad_k, dot(g, rounded, TN).T
 
 
 def position(index):
-    group = sum(jnp.where(index >= n * GROUP, 1, 0) for n in range(1, GROUPS))
-    inner = index - group * GROUP
-    rest = inner - BLOCK
-    near = (inner >> 3) * 16 + (inner & 7)
+    rest = index - BLOCK
+    near = (index >> 3) * 16 + (index & 7)
     far = (rest >> 2) * 16 + 8 + (rest & 3)
-    return group * 512 + jnp.where(inner < BLOCK, near, far)
+    return jnp.where(index < BLOCK, near, far)
 
 
 def routed_kernel(
@@ -284,7 +292,9 @@
         here = slice(i * GROUP, (i + 1) * GROUP)
         upto = slice(0, (i + 1) * GROUP)
         same = name_col_ref[here, :] == name_row_ref[:, upto]
-        past = position(iota((1, (i + 1) * GROUP), 1)) <= position(iota((GROUP, 1), 0) + i * GROUP)
+        past = position(iota((1, GROUP), 1)) <= position(iota((GROUP, 1), 0))
+        if i:
+            past = jnp.concatenate([jnp.full((GROUP, i * GROUP), True), past], axis=1)
         out, gq, gk, gv = attend(
             rows[here, 0:HD],
             rows[upto, HD : 2 * HD],
@@ -410,16 +420,19 @@
     )(keys, values)
     steps = [(s, s + 1) for s in range(DEVS - 1)]
     halo = lax.ppermute(tail, "seq", steps)
-    counts, within = call(
+    counts = call(
         count_kernel,
-        (shape((DEVS, 8, 128)), shape((8, TOK), F32)),
+        shape((DEVS, 8, 128)),
         [VMEM],
-        (VMEM,) * 2,
-        flops=2 * 2 * TOK**3,
-        moved=2**20,
+        VMEM,
+        flops=2 * 2 * 8 * TOK**2,
+        moved=2**18,
     )(labels)
     counts = lax.all_to_all(counts, "seq", split_axis=0, concat_axis=0, tiled=True)
-    counts, halo = lax.optimization_barrier((counts, halo))
+    within = call(
+        rank_kernel, shape((8, TOK), F32), [VMEM], VMEM, flops=2 * 2 * TOK**3, moved=2**15
+    )(labels)
+    counts, halo, within = lax.optimization_barrier((counts, halo, within))
 
     def window(halo):
         return call(

time: 236 us -> 236 us (level)
  no operation moved by 1% of the time
where the time goes in v3:
time: 236 us; the launch traced here: 235 us
  waiting for transfers between devices  155 us (66%)
  starting transfers between devices  47.9 us (20%)
  Pallas kernels  29.2 us (12%)
    all_to_all x2, waiting for transfers between devices, across(): lax.all_to_all(blocks, 'seq', split_axis=0, concat_axis=0, tiled=True)  126 us
    all_to_all x1, starting transfers between devices, local(): lax.all_to_all(counts, 'seq', split_axis=0, concat_axis=0, tiled=True)  19.9 us
    all_to_all x2, starting transfers between devices, across(): lax.all_to_all(blocks, 'seq', split_axis=0, concat_axis=0, tiled=True)  17 us
    all_to_all x1, waiting for transfers between devices, local(): lax.all_to_all(counts, 'seq', split_axis=0, concat_axis=0, tiled=True)  13.9 us
    pallas_call x1, Pallas kernels, serve(): call(routed_kernel, shape((NEAR, WIDE)), [VMEM] * 3, ANY, scratch=(pltpu....  8.34 us
    pallas_call x1, Pallas kernels, serve(): call(place_kernel, (shape((NEAR, WIDE)), shape((8, TOK), jnp.int32), shap...  6.31 us
    ppermute x1, waiting for transfers between devices, serve(): edge = lax.ppermute(edge, 'seq', [(b, a) for a, b in steps])  6.05 us
    pallas_call x1, Pallas kernels, window(): call(window_kernel, (full, full, shape((TOK, half), F32), shape((TOK, hal...  5.78 us
  transfers between devices with their start and end apart: 7, of which 7 were waited for; matrix products, arithmetic and copies ran while one was open for 1% of the time, Pallas kernels for 4%

profile of v3, /device:TPU:39, one launch (start us, length us, event | category | flops | bytes accessed | tf_op | source)
XLA Modules:
  0.0 234.9 jit_solution(11394318268794752569)
XLA Ops:
  0.6 0.0 copy-start.1
  0.6 1.9 shard_map.84
  2.5 19.9 %all-to-all-start.2 = ((bf16[128,8,128]{2,1,0:T(8,128)(2,1)}), bf16[128,8,128]{2,1,0:T(8,128)(2,1)}, u32[]{:S(2)}, u32[]{:S(2)}) async-start(bf16[128,8,128]{2,1,0:T(8,128)(2,1)} %shard_map.84), calls=%async_computation.2 | async-start | bytes 524288 | tf_op jit(solution)/shard_map/all_to_all | solution.py:431
  22.5 1.1 shard_map.85
  23.5 3.3 %collective-permute-start = (bf16[256,512]{1,0:T(8,128)(2,1)S(1)}, bf16[256,512]{1,0:T(8,128)(2,1)S(1)}, u32[]{:S(2)}, u32[]{:S(2)}) collective-permute-start(bf16[256,512]{1,0:T(8,128)(2,1)S(1)} %shard_map.85), channel_id=1, source_target_pairs={{0,4},{4,8},{8,12},{12,16},{16,20},{20,24},{24,28},{28,32},{32,36}... | collective-permute-start | bytes 786440 | tf_op jit(solution)/shard_map/ppermute | solution.py:422
  26.9 0.0 copy-done.1
  26.9 0.8 shard_map.86.within_ref
  27.7 0.1 pad_add_fusion.1.where_ref
  27.8 3.0 %collective-permute-done.halo_ref = bf16[256,512]{1,0:T(8,128)(2,1)S(1)} collective-permute-done((bf16[256,512]{1,0:T(8,128)(2,1)S(1)}, bf16[256,512]{1,0:T(8,128)(2,1)S(1)}, u32[]{:S(2)}, u32[]{:S(2)}) %collective-permute-start) | collective-permute-done | bytes 262176 | tf_op jit(solution)/shard_map/ppermute | solution.py:422
  30.8 13.9 %all-to-all-done.2.counts_ref = bf16[128,8,128]{2,1,0:T(8,128)(2,1)} async-done(((bf16[128,8,128]{2,1,0:T(8,128)(2,1)}), bf16[128,8,128]{2,1,0:T(8,128)(2,1)}, u32[]{:S(2)}, u32[]{:S(2)}) %all-to-all-start.2) | async-done | bytes 262176 | tf_op jit(solution)/shard_map/all_to_all | solution.py:431
  44.7 6.3 %shard_map.87 = (bf16[1024,768]{1,0:T(8,128)(2,1)}, s32[8,512]{1,0:T(8,128)S(1)}, s32[128,16]{1,0:T(8,128)S(1)}, f32[8,128]{1,0:T(8,128)S(1)}) custom-call(s32[2]{0:T(128)S(1)} %pad_add_fusion.1.where_ref, bf16[128,8,128]{2,1,0:T(8,128)(2,1)} %all-to-all-done.2.counts_ref, s32[2,1,512]{2,1,0:T(1,128)S(1)} %bitcast.65, f32[8,512]{1,0:T(8,128)S(1)} %shard_map.86.within_ref, ...), custom_call_target="tpu_custom_call" | custom-call | flops 1610612736 | bytes 6291456 | tf_op jit(solution)/shard_map/pallas_call | solution.py:454
  51.0 8.0 %all-to-all-start.3 = ((bf16[128,8,768]{2,1,0:T(8,128)(2,1)}), bf16[128,8,768]{2,1,0:T(8,128)(2,1)S(1)}, u32[]{:S(2)}, u32[]{:S(2)}) async-start(bf16[128,8,768]{2,1,0:T(8,128)(2,1)} %bitcast.8), calls=%async_computation.3 | async-start | bytes 3145728 | tf_op jit(solution)/shard_map/all_to_all | solution.py:402
  59.0 5.8 %shard_map.88 = (bf16[512,512]{1,0:T(8,128)(2,1)}, bf16[512,512]{1,0:T(8,128)(2,1)}, f32[512,256]{1,0:T(8,128)S(1)}, f32[512,256]{1,0:T(8,128)S(1)}, bf16[256,512]{1,0:T(8,128)(2,1)}) custom-call(s32[1]{0:T(128)} %bitcast.6.where_ref, bf16[512,512]{1,0:T(8,128)(2,1)} %q_ref.3, bf16[512,512]{1,0:T(8,128)(2,1)} %k_ref.5, bf16[512,512]{1,0:T(8,128)(2,1)} %v_ref.5, ...), custom_call_target="tpu_custom_call" | custom-call | flops 805306368 | bytes 6291456 | tf_op jit(solution)/shard_map/pallas_call | solution.py:438
  64.8 2.5 %collective-permute-start.1 = (bf16[256,512]{1,0:T(8,128)(2,1)}, bf16[256,512]{1,0:T(8,128)(2,1)}, u32[]{:S(2)}, u32[]{:S(2)}) collective-permute-start(bf16[256,512]{1,0:T(8,128)(2,1)} %get-tuple-element.116), channel_id=1, source_target_pairs={{4,0},{8,4},{12,8},{16,12},{20,16},{24,20},{28,24},{32,28},{36,32}... | collective-permute-start | bytes 786440 | tf_op jit(solution)/shard_map/ppermute | solution.py:479
  67.3 0.1 slice.16
  67.4 0.1 reshape.69
  67.5 0.1 reshape.68
  67.7 0.3 copy.19
  68.0 6.0 %collective-permute-done.1.edge_ref = bf16[256,512]{1,0:T(8,128)(2,1)} collective-permute-done((bf16[256,512]{1,0:T(8,128)(2,1)}, bf16[256,512]{1,0:T(8,128)(2,1)}, u32[]{:S(2)}, u32[]{:S(2)}) %collective-permute-start.1) | collective-permute-done | bytes 262176 | tf_op jit(solution)/shard_map/ppermute | solution.py:479
  74.0 62.5 %all-to-all-done.3 = bf16[128,8,768]{2,1,0:T(8,128)(2,1)S(1)} async-done(((bf16[128,8,768]{2,1,0:T(8,128)(2,1)}), bf16[128,8,768]{2,1,0:T(8,128)(2,1)S(1)}, u32[]{:S(2)}, u32[]{:S(2)}) %all-to-all-start.3) | async-done | bytes 1572896 | tf_op jit(solution)/shard_map/all_to_all | solution.py:402
  136.5 8.3 %shard_map.89 = bf16[1024,768]{1,0:T(8,128)(2,1)} custom-call(bf16[1024,768]{1,0:T(8,128)(2,1)S(1)} %bitcast.54, s32[1536,1]{1,0:T(8,128)S(1)} %bitcast.55, s32[1,1536]{1,0:T(1,128)S(1)} %bitcast.60), custom_call_target="tpu_custom_call" | custom-call | flops 1811939328 | bytes 4194304 | tf_op jit(solution)/shard_map/pallas_call | solution.py:484
  144.9 9.0 %all-to-all-start.4 = ((bf16[128,8,768]{2,1,0:T(8,128)(2,1)}), bf16[128,8,768]{2,1,0:T(8,128)(2,1)S(1)}, u32[]{:S(2)}, u32[]{:S(2)}) async-start(bf16[128,8,768]{2,1,0:T(8,128)(2,1)} %bitcast.10), calls=%async_computation.4 | async-start | bytes 3145728 | tf_op jit(solution)/shard_map/all_to_all | solution.py:402
  153.9 2.1 collective-permute-start.2
  156.0 2.5 %collective-permute-done.2 = f32[8,128]{1,0:T(8,128)S(1)} collective-permute-done((f32[8,128]{1,0:T(8,128)S(1)}, f32[8,128]{1,0:T(8,128)S(1)}, u32[]{:S(2)}, u32[]{:S(2)}) %collective-permute-start.2) | collective-permute-done | bytes 4128 | tf_op jit(solution)/shard_map/ppermute | solution.py:506
  158.5 3.0 %collective-permute-start.3 = (f32[8,128]{1,0:T(8,128)S(1)}, f32[8,128]{1,0:T(8,128)S(1)}, u32[]{:S(2)}, u32[]{:S(2)}) collective-permute-start(f32[8,128]{1,0:T(8,128)S(1)} %max.6), channel_id=1, source_target_pairs={{0,2},{1,3},{2,0},{3,1},{4,6},{5,7},{6,4},{7,5},{8,10},{9,11},{10,... | collective-permute-start | bytes 12296 | tf_op jit(solution)/shard_map/ppermute | solution.py:506
  161.6 3.1 %collective-permute-done.3 = f32[8,128]{1,0:T(8,128)S(1)} collective-permute-done((f32[8,128]{1,0:T(8,128)S(1)}, f32[8,128]{1,0:T(8,128)S(1)}, u32[]{:S(2)}, u32[]{:S(2)}) %collective-permute-start.3) | collective-permute-done | bytes 4128 | tf_op jit(solution)/shard_map/ppermute | solution.py:506
  164.7 0.5 slice.17
  165.8 2.0 shard_map.90
  167.8 63.6 %all-to-all-done.4 = bf16[128,8,768]{2,1,0:T(8,128)(2,1)S(1)} async-done(((bf16[128,8,768]{2,1,0:T(8,128)(2,1)}), bf16[128,8,768]{2,1,0:T(8,128)(2,1)S(1)}, u32[]{:S(2)}, u32[]{:S(2)}) %all-to-all-start.4) | async-done | bytes 1572896 | tf_op jit(solution)/shard_map/all_to_all | solution.py:402
  231.4 3.1 %shard_map.91 = (bf16[512,512]{1,0:T(8,128)(2,1)}, bf16[512,512]{1,0:T(8,128)(2,1)}, bf16[512,512]{1,0:T(8,128)(2,1)}, bf16[512,512]{1,0:T(8,128)(2,1)}) custom-call(s32[8,512]{1,0:T(8,128)S(1)} %get-tuple-element.111.slot_ref, bf16[1024,768]{1,0:T(8,128)(2,1)S(1)} %bitcast.53, ...), custom_call_target="tpu_custom_call", output_to_operand_aliasing={{0}: (2, {}), {1}: (3, {}), {2}: (4, {}), {3}: (5, {})} | custom-call | flops 1610612736 | bytes 6291456 | tf_op jit(solution)/shard_map/pallas_call | solution.py:511
  234.5 0.2 while.16
  (5 shorter events, 0.0 us)
Async XLA Ops:
  0.6 26.2 %copy-start.1 = (s32[2,512,1]{1,2,0:T(1,128)S(1)}, s32[2,512,1]{1,2,0:T(1,128)}, u32[]{:S(2)}) copy-start(s32[2,512,1]{1,2,0:T(1,128)} %param.11) | copy-start | bytes 12292
  2.5 42.2 %all-to-all-start.2 = ((bf16[128,8,128]{2,1,0:T(8,128)(2,1)}), bf16[128,8,128]{2,1,0:T(8,128)(2,1)}, u32[]{:S(2)}, u32[]{:S(2)}) async-start(bf16[128,8,128]{2,1,0:T(8,128)(2,1)} %shard_map.84), calls=%async_computation.2 | async-start | bytes 524288 | tf_op jit(solution)/shard_map/all_to_all | solution.py:431
  23.5 7.3 %collective-permute-start = (bf16[256,512]{1,0:T(8,128)(2,1)S(1)}, bf16[256,512]{1,0:T(8,128)(2,1)S(1)}, u32[]{:S(2)}, u32[]{:S(2)}) collective-permute-start(bf16[256,512]{1,0:T(8,128)(2,1)S(1)} %shard_map.85), channel_id=1, source_target_pairs={{0,4},{4,8},{8,12},{12,16},{16,20},{20,24},{24,28},{28,32},{32,36}... | collective-permute-start | bytes 786440 | tf_op jit(solution)/shard_map/ppermute | solution.py:422
  51.0 85.6 %all-to-all-start.3 = ((bf16[128,8,768]{2,1,0:T(8,128)(2,1)}), bf16[128,8,768]{2,1,0:T(8,128)(2,1)S(1)}, u32[]{:S(2)}, u32[]{:S(2)}) async-start(bf16[128,8,768]{2,1,0:T(8,128)(2,1)} %bitcast.8), calls=%async_computation.3 | async-start | bytes 3145728 | tf_op jit(solution)/shard_map/all_to_all | solution.py:402
  64.8 9.2 %collective-permute-start.1 = (bf16[256,512]{1,0:T(8,128)(2,1)}, bf16[256,512]{1,0:T(8,128)(2,1)}, u32[]{:S(2)}, u32[]{:S(2)}) collective-permute-start(bf16[256,512]{1,0:T(8,128)(2,1)} %get-tuple-element.116), channel_id=1, source_target_pairs={{4,0},{8,4},{12,8},{16,12},{20,16},{24,20},{28,24},{32,28},{36,32}... | collective-permute-start | bytes 786440 | tf_op jit(solution)/shard_map/ppermute | solution.py:479
  144.9 86.5 %all-to-all-start.4 = ((bf16[128,8,768]{2,1,0:T(8,128)(2,1)}), bf16[128,8,768]{2,1,0:T(8,128)(2,1)S(1)}, u32[]{:S(2)}, u32[]{:S(2)}) async-start(bf16[128,8,768]{2,1,0:T(8,128)(2,1)} %bitcast.10), calls=%async_computation.4 | async-start | bytes 3145728 | tf_op jit(solution)/shard_map/all_to_all | solution.py:402
  153.9 4.6 %collective-permute-start.2 = (f32[8,128]{1,0:T(8,128)S(1)}, f32[8,128]{1,0:T(8,128)S(1)}, u32[]{:S(2)}, u32[]{:S(2)}) collective-permute-start(f32[8,128]{1,0:T(8,128)S(1)} %get-tuple-element.130), channel_id=1, source_target_pairs={{0,1},{1,2},{2,3},{3,0},{4,5},{5,6},{6,7},{7,4},{8,9},{9,10},{10,1... | collective-permute-start | bytes 12296 | tf_op jit(solution)/shard_map/ppermute | solution.py:506
  158.5 6.1 %collective-permute-start.3 = (f32[8,128]{1,0:T(8,128)S(1)}, f32[8,128]{1,0:T(8,128)S(1)}, u32[]{:S(2)}, u32[]{:S(2)}) collective-permute-start(f32[8,128]{1,0:T(8,128)S(1)} %max.6), channel_id=1, source_target_pairs={{0,2},{1,3},{2,0},{3,1},{4,6},{5,7},{6,4},{7,5},{8,10},{9,11},{10,... | collective-permute-start | bytes 12296 | tf_op jit(solution)/shard_map/ppermute | solution.py:506

commit v4 on v3

--- a/solution.py
+++ b/solution.py
@@ -353,12 +353,11 @@
         ref[TOK - WINDOW :, 0:half] = (mine[TOK - WINDOW :, :] + edge.astype(F32)).astype(BF)
 
 
-def fetch(slot_ref, rows_ref, h, i):
-    part = slice(i * BLOCK, (i + 1) * BLOCK)
-    spot = slot_ref[h : h + 1, part].astype(F32)
-    spot = jnp.broadcast_to(spot, (128, BLOCK)).T[:, 0:1].astype(jnp.int32)
-    pick = ones_where(iota((BLOCK, ROWS), 1) == spot).astype(BF)
-    return part, dot(pick, rows_ref[...])
+def fetch(slot_ref, rows_ref, h):
+    spot = slot_ref[h : h + 1, :].astype(F32)
+    spot = jnp.broadcast_to(spot, (128, TOK)).T[:, 0:1].astype(jnp.int16)
+    lane = lax.broadcasted_iota(jnp.int16, (TOK, ROWS), 1)
+    return dot(jnp.where(lane == spot, BF(1), BF(0)), rows_ref[...])
 
 
 def finish_kernel(slot_ref, back_ref, *refs):
@@ -366,16 +365,12 @@
     rows, stage, sems = refs[8:]
     spread_out(back_ref, rows)
     copies = []
-    for i in range(TOK // BLOCK):
-        for h in range(2):
-            part, found = fetch(slot_ref, rows, h, i)
-            for n in range(4):
-                stage[n, part, h * HD : (h + 1) * HD] = found[:, n * HD : (n + 1) * HD].astype(BF)
+    for h in range(2):
+        found = fetch(slot_ref, rows, h).astype(BF)
         for n in range(4):
+            stage[n, h] = found[:, n * HD : (n + 1) * HD]
             copy = pltpu.make_async_copy(
-                stage.at[n, pl.ds(i * BLOCK, BLOCK), :],
-                outs[n].at[pl.ds(i * BLOCK, BLOCK), pl.ds(2 * HD, 2 * HD)],
-                sems.at[n, i],
+                stage.at[n, h], outs[n].at[:, pl.ds((2 + h) * HD, HD)], sems.at[n, h]
             )
             copy.start()
             copies.append(copy)
@@ -386,15 +381,14 @@
 def add_kernel(slot_ref, back_ref, *refs):
     before, after, rows = refs[0:4], refs[4:8], refs[8]
     spread_out(back_ref, rows)
+    for n in range(4):
+        after[n][:, 0 : 2 * HD] = before[n][:, 0 : 2 * HD]
     for h in range(2):
         to = slice((2 + h) * HD, (3 + h) * HD)
-        for i in range(TOK // BLOCK):
-            part, found = fetch(slot_ref, rows, h, i)
-            for n in range(4):
-                if h == 0:
-                    after[n][part, 0 : 2 * HD] = before[n][part, 0 : 2 * HD]
-                more = before[n][part, to].astype(F32) + found[:, n * HD : (n + 1) * HD]
-                after[n][part, to] = more.astype(BF)
+        found = fetch(slot_ref, rows, h)
+        for n in range(4):
+            more = before[n][:, to].astype(F32) + found[:, n * HD : (n + 1) * HD]
+            after[n][:, to] = more.astype(BF)
 
 
 def across(rows):
@@ -515,8 +509,8 @@
         (ANY,) * 4,
         scratch=(
             rows_scratch,
-            pltpu.VMEM((4, TOK, half), BF),
-            pltpu.SemaphoreType.DMA((4, TOK // BLOCK)),
+            pltpu.VMEM((4, 2, TOK, HD), BF),
+            pltpu.SemaphoreType.DMA((4, 2)),
         ),
         flops=2 * 2 * ROWS * TOK * TOK,
         moved=6 * 2**20,

time: 236 us -> 236 us (level)
  no operation moved by 1% of the time
where the time goes in v4:
time: 236 us; the launch traced here: 235 us
  waiting for transfers between devices  156 us (66%)
  starting transfers between devices  47 us (20%)
  Pallas kernels  29.8 us (13%)
    all_to_all x2, waiting for transfers between devices, across(): lax.all_to_all(blocks, 'seq', split_axis=0, concat_axis=0, tiled=True)  126 us
    all_to_all x1, starting transfers between devices, local(): lax.all_to_all(counts, 'seq', split_axis=0, concat_axis=0, tiled=True)  19.9 us
    all_to_all x2, starting transfers between devices, across(): lax.all_to_all(blocks, 'seq', split_axis=0, concat_axis=0, tiled=True)  17 us
    all_to_all x1, waiting for transfers between devices, local(): lax.all_to_all(counts, 'seq', split_axis=0, concat_axis=0, tiled=True)  13.9 us
    pallas_call x1, Pallas kernels, serve(): call(routed_kernel, shape((NEAR, WIDE)), [VMEM] * 3, ANY, scratch=(pltpu....  8.35 us
    pallas_call x1, Pallas kernels, serve(): call(place_kernel, (shape((NEAR, WIDE)), shape((8, TOK), jnp.int32), shap...  7.03 us
    ppermute x2, waiting for transfers between devices, local(): over = jnp.maximum(over, lax.ppermute(over, 'head', turn))  6.53 us
    ppermute x1, waiting for transfers between devices, serve(): edge = lax.ppermute(edge, 'seq', [(b, a) for a, b in steps])  6.08 us
  transfers between devices with their start and end apart: 7, of which 7 were waited for; matrix products, arithmetic and copies ran while one was open for 1% of the time, Pallas kernels for 4%

profile of v4, /device:TPU:39, one launch (start us, length us, event | category | flops | bytes accessed | tf_op | source)
XLA Modules:
  0.0 235.5 jit_solution(6815693940174982042)
XLA Ops:
  0.6 0.0 copy-start.1
  0.6 1.9 shard_map.84
  2.5 19.9 %all-to-all-start.2 = ((bf16[128,8,128]{2,1,0:T(8,128)(2,1)}), bf16[128,8,128]{2,1,0:T(8,128)(2,1)}, u32[]{:S(2)}, u32[]{:S(2)}) async-start(bf16[128,8,128]{2,1,0:T(8,128)(2,1)} %shard_map.84), calls=%async_computation.2 | async-start | bytes 524288 | tf_op jit(solution)/shard_map/all_to_all | solution.py:425
  22.5 1.1 shard_map.85
  23.5 3.3 %collective-permute-start = (bf16[256,512]{1,0:T(8,128)(2,1)S(1)}, bf16[256,512]{1,0:T(8,128)(2,1)S(1)}, u32[]{:S(2)}, u32[]{:S(2)}) collective-permute-start(bf16[256,512]{1,0:T(8,128)(2,1)S(1)} %shard_map.85), channel_id=1, source_target_pairs={{0,4},{4,8},{8,12},{12,16},{16,20},{20,24},{24,28},{28,32},{32,36}... | collective-permute-start | bytes 786440 | tf_op jit(solution)/shard_map/ppermute | solution.py:416
  26.9 0.0 copy-done.1
  26.9 0.8 shard_map.86.within_ref
  27.7 0.1 pad_add_fusion.1.where_ref
  27.8 3.0 %collective-permute-done.halo_ref = bf16[256,512]{1,0:T(8,128)(2,1)S(1)} collective-permute-done((bf16[256,512]{1,0:T(8,128)(2,1)S(1)}, bf16[256,512]{1,0:T(8,128)(2,1)S(1)}, u32[]{:S(2)}, u32[]{:S(2)}) %collective-permute-start) | collective-permute-done | bytes 262176 | tf_op jit(solution)/shard_map/ppermute | solution.py:416
  30.8 13.9 %all-to-all-done.2.counts_ref = bf16[128,8,128]{2,1,0:T(8,128)(2,1)} async-done(((bf16[128,8,128]{2,1,0:T(8,128)(2,1)}), bf16[128,8,128]{2,1,0:T(8,128)(2,1)}, u32[]{:S(2)}, u32[]{:S(2)}) %all-to-all-start.2) | async-done | bytes 262176 | tf_op jit(solution)/shard_map/all_to_all | solution.py:425
  44.7 7.0 %shard_map.87 = (bf16[1024,768]{1,0:T(8,128)(2,1)}, s32[8,512]{1,0:T(8,128)S(1)}, s32[128,16]{1,0:T(8,128)S(1)}, f32[8,128]{1,0:T(8,128)S(1)}) custom-call(s32[2]{0:T(128)S(1)} %pad_add_fusion.1.where_ref, bf16[128,8,128]{2,1,0:T(8,128)(2,1)} %all-to-all-done.2.counts_ref, s32[2,1,512]{2,1,0:T(1,128)S(1)} %bitcast.65, f32[8,512]{1,0:T(8,128)S(1)} %shard_map.86.within_ref, ...), custom_call_target="tpu_custom_call" | custom-call | flops 1610612736 | bytes 6291456 | tf_op jit(solution)/shard_map/pallas_call | solution.py:448
  51.7 8.0 %all-to-all-start.3 = ((bf16[128,8,768]{2,1,0:T(8,128)(2,1)}), bf16[128,8,768]{2,1,0:T(8,128)(2,1)S(1)}, u32[]{:S(2)}, u32[]{:S(2)}) async-start(bf16[128,8,768]{2,1,0:T(8,128)(2,1)} %bitcast.8), calls=%async_computation.3 | async-start | bytes 3145728 | tf_op jit(solution)/shard_map/all_to_all | solution.py:396
  59.7 5.8 %shard_map.88 = (bf16[512,512]{1,0:T(8,128)(2,1)}, bf16[512,512]{1,0:T(8,128)(2,1)}, f32[512,256]{1,0:T(8,128)S(1)}, f32[512,256]{1,0:T(8,128)S(1)}, bf16[256,512]{1,0:T(8,128)(2,1)}) custom-call(s32[1]{0:T(128)} %bitcast.6.where_ref, bf16[512,512]{1,0:T(8,128)(2,1)} %q_ref.3, bf16[512,512]{1,0:T(8,128)(2,1)} %k_ref.5, bf16[512,512]{1,0:T(8,128)(2,1)} %v_ref.5, ...), custom_call_target="tpu_custom_call" | custom-call | flops 805306368 | bytes 6291456 | tf_op jit(solution)/shard_map/pallas_call | solution.py:432
  65.5 2.5 %collective-permute-start.1 = (bf16[256,512]{1,0:T(8,128)(2,1)}, bf16[256,512]{1,0:T(8,128)(2,1)}, u32[]{:S(2)}, u32[]{:S(2)}) collective-permute-start(bf16[256,512]{1,0:T(8,128)(2,1)} %get-tuple-element.116), channel_id=1, source_target_pairs={{4,0},{8,4},{12,8},{16,12},{20,16},{24,20},{28,24},{32,28},{36,32}... | collective-permute-start | bytes 786440 | tf_op jit(solution)/shard_map/ppermute | solution.py:473
  68.1 0.1 slice.16
  68.1 0.1 reshape.69
  68.3 0.1 reshape.68
  68.4 0.3 copy.19
  68.7 6.1 %collective-permute-done.1.edge_ref = bf16[256,512]{1,0:T(8,128)(2,1)} collective-permute-done((bf16[256,512]{1,0:T(8,128)(2,1)}, bf16[256,512]{1,0:T(8,128)(2,1)}, u32[]{:S(2)}, u32[]{:S(2)}) %collective-permute-start.1) | collective-permute-done | bytes 262176 | tf_op jit(solution)/shard_map/ppermute | solution.py:473
  74.8 62.5 %all-to-all-done.3 = bf16[128,8,768]{2,1,0:T(8,128)(2,1)S(1)} async-done(((bf16[128,8,768]{2,1,0:T(8,128)(2,1)}), bf16[128,8,768]{2,1,0:T(8,128)(2,1)S(1)}, u32[]{:S(2)}, u32[]{:S(2)}) %all-to-all-start.3) | async-done | bytes 1572896 | tf_op jit(solution)/shard_map/all_to_all | solution.py:396
  137.2 8.3 %shard_map.89 = bf16[1024,768]{1,0:T(8,128)(2,1)} custom-call(bf16[1024,768]{1,0:T(8,128)(2,1)S(1)} %bitcast.54, s32[1536,1]{1,0:T(8,128)S(1)} %bitcast.55, s32[1,1536]{1,0:T(1,128)S(1)} %bitcast.60), custom_call_target="tpu_custom_call" | custom-call | flops 1811939328 | bytes 4194304 | tf_op jit(solution)/shard_map/pallas_call | solution.py:478
  145.6 9.0 %all-to-all-start.4 = ((bf16[128,8,768]{2,1,0:T(8,128)(2,1)}), bf16[128,8,768]{2,1,0:T(8,128)(2,1)S(1)}, u32[]{:S(2)}, u32[]{:S(2)}) async-start(bf16[128,8,768]{2,1,0:T(8,128)(2,1)} %bitcast.10), calls=%async_computation.4 | async-start | bytes 3145728 | tf_op jit(solution)/shard_map/all_to_all | solution.py:396
  154.6 1.9 collective-permute-start.2
  156.5 2.7 %collective-permute-done.2 = f32[8,128]{1,0:T(8,128)S(1)} collective-permute-done((f32[8,128]{1,0:T(8,128)S(1)}, f32[8,128]{1,0:T(8,128)S(1)}, u32[]{:S(2)}, u32[]{:S(2)}) %collective-permute-start.2) | collective-permute-done | bytes 4128 | tf_op jit(solution)/shard_map/ppermute | solution.py:500
  159.2 2.3 collective-permute-start.3
  161.6 3.8 %collective-permute-done.3 = f32[8,128]{1,0:T(8,128)S(1)} collective-permute-done((f32[8,128]{1,0:T(8,128)S(1)}, f32[8,128]{1,0:T(8,128)S(1)}, u32[]{:S(2)}, u32[]{:S(2)}) %collective-permute-start.3) | collective-permute-done | bytes 4128 | tf_op jit(solution)/shard_map/ppermute | solution.py:500
  165.4 0.5 slice.17
  166.5 2.0 shard_map.90
  168.5 63.6 %all-to-all-done.4 = bf16[128,8,768]{2,1,0:T(8,128)(2,1)S(1)} async-done(((bf16[128,8,768]{2,1,0:T(8,128)(2,1)}), bf16[128,8,768]{2,1,0:T(8,128)(2,1)S(1)}, u32[]{:S(2)}, u32[]{:S(2)}) %all-to-all-start.4) | async-done | bytes 1572896 | tf_op jit(solution)/shard_map/all_to_all | solution.py:396
  232.1 3.0 %shard_map.91 = (bf16[512,512]{1,0:T(8,128)(2,1)}, bf16[512,512]{1,0:T(8,128)(2,1)}, bf16[512,512]{1,0:T(8,128)(2,1)}, bf16[512,512]{1,0:T(8,128)(2,1)}) custom-call(s32[8,512]{1,0:T(8,128)S(1)} %get-tuple-element.111.slot_ref, bf16[1024,768]{1,0:T(8,128)(2,1)S(1)} %bitcast.53, ...), custom_call_target="tpu_custom_call", output_to_operand_aliasing={{0}: (2, {}), {1}: (3, {}), {2}: (4, {}), {3}: (5, {})} | custom-call | flops 1610612736 | bytes 6291456 | tf_op jit(solution)/shard_map/pallas_call | solution.py:505
  235.1 0.2 while.16
  (5 shorter events, 0.0 us)
Async XLA Ops:
  0.6 26.2 %copy-start.1 = (s32[2,512,1]{1,2,0:T(1,128)S(1)}, s32[2,512,1]{1,2,0:T(1,128)}, u32[]{:S(2)}) copy-start(s32[2,512,1]{1,2,0:T(1,128)} %param.11) | copy-start | bytes 12292
  2.5 42.2 %all-to-all-start.2 = ((bf16[128,8,128]{2,1,0:T(8,128)(2,1)}), bf16[128,8,128]{2,1,0:T(8,128)(2,1)}, u32[]{:S(2)}, u32[]{:S(2)}) async-start(bf16[128,8,128]{2,1,0:T(8,128)(2,1)} %shard_map.84), calls=%async_computation.2 | async-start | bytes 524288 | tf_op jit(solution)/shard_map/all_to_all | solution.py:425
  23.5 7.3 %collective-permute-start = (bf16[256,512]{1,0:T(8,128)(2,1)S(1)}, bf16[256,512]{1,0:T(8,128)(2,1)S(1)}, u32[]{:S(2)}, u32[]{:S(2)}) collective-permute-start(bf16[256,512]{1,0:T(8,128)(2,1)S(1)} %shard_map.85), channel_id=1, source_target_pairs={{0,4},{4,8},{8,12},{12,16},{16,20},{20,24},{24,28},{28,32},{32,36}... | collective-permute-start | bytes 786440 | tf_op jit(solution)/shard_map/ppermute | solution.py:416
  51.7 85.5 %all-to-all-start.3 = ((bf16[128,8,768]{2,1,0:T(8,128)(2,1)}), bf16[128,8,768]{2,1,0:T(8,128)(2,1)S(1)}, u32[]{:S(2)}, u32[]{:S(2)}) async-start(bf16[128,8,768]{2,1,0:T(8,128)(2,1)} %bitcast.8), calls=%async_computation.3 | async-start | bytes 3145728 | tf_op jit(solution)/shard_map/all_to_all | solution.py:396
  65.5 9.3 %collective-permute-start.1 = (bf16[256,512]{1,0:T(8,128)(2,1)}, bf16[256,512]{1,0:T(8,128)(2,1)}, u32[]{:S(2)}, u32[]{:S(2)}) collective-permute-start(bf16[256,512]{1,0:T(8,128)(2,1)} %get-tuple-element.116), channel_id=1, source_target_pairs={{4,0},{8,4},{12,8},{16,12},{20,16},{24,20},{28,24},{32,28},{36,32}... | collective-permute-start | bytes 786440 | tf_op jit(solution)/shard_map/ppermute | solution.py:473
  145.6 86.5 %all-to-all-start.4 = ((bf16[128,8,768]{2,1,0:T(8,128)(2,1)}), bf16[128,8,768]{2,1,0:T(8,128)(2,1)S(1)}, u32[]{:S(2)}, u32[]{:S(2)}) async-start(bf16[128,8,768]{2,1,0:T(8,128)(2,1)} %bitcast.10), calls=%async_computation.4 | async-start | bytes 3145728 | tf_op jit(solution)/shard_map/all_to_all | solution.py:396
  154.6 4.6 %collective-permute-start.2 = (f32[8,128]{1,0:T(8,128)S(1)}, f32[8,128]{1,0:T(8,128)S(1)}, u32[]{:S(2)}, u32[]{:S(2)}) collective-permute-start(f32[8,128]{1,0:T(8,128)S(1)} %get-tuple-element.130), channel_id=1, source_target_pairs={{0,1},{1,2},{2,3},{3,0},{4,5},{5,6},{6,7},{7,4},{8,9},{9,10},{10,1... | collective-permute-start | bytes 12296 | tf_op jit(solution)/shard_map/ppermute | solution.py:500
  159.2 6.1 %collective-permute-start.3 = (f32[8,128]{1,0:T(8,128)S(1)}, f32[8,128]{1,0:T(8,128)S(1)}, u32[]{:S(2)}, u32[]{:S(2)}) collective-permute-start(f32[8,128]{1,0:T(8,128)S(1)} %max.6), channel_id=1, source_target_pairs={{0,2},{1,3},{2,0},{3,1},{4,6},{5,7},{6,4},{7,5},{8,10},{9,11},{10,... | collective-permute-start | bytes 12296 | tf_op jit(solution)/shard_map/ppermute | solution.py:500
